TPU v7x, 256 devices: a whole 4x4x8 slice. The times are simulated.
256 devices in a mesh: users: 128 (over z, x, y), rep: 2 (over core).
Axes of the slice: x: 4, y: 4, z: 8, core: 2. Of those that a mesh axis runs over, the one named last changes fastest.
Arguments:
- user_factors: float32 [131072, 256], P('users'), may hold values from -1.5 to 1.5
- user_accum: float32 [131072, 256], P('users'), may hold values from 0.5 to 8
- item_factors: float32 [32768, 256], P('users'), may hold values from -1.5 to 1.5
- item_accum: float32 [32768, 256], P('users'), may hold values from 0.5 to 8
- tile_counts: bfloat16 [128, 2, 128, 128, 128], P('users', 'rep'), may hold values from 0 to 20, as said below
- tile_user: int32 [128, 2, 128], P('users', 'rep'), may hold values from 0 to 7
- tile_item: int32 [128, 2, 128], P('users', 'rep'), may hold values from 0 to 255, as said below
- send_list: int32 [128, 2, 128], P('users', 'rep'), may hold values from 0 to 2, as said below
Outputs:
- new_users: float32 [131072, 256], P('users')
- new_user_accum: float32 [131072, 256], P('users')
- new_items: float32 [32768, 256], P('users')
- new_item_accum: float32 [32768, 256], P('users')
Inputs may be any that keep to these rules, and one draw needn't show every extreme that they name: `tile_counts`: zero means no interaction. `tile_item`: panel b belongs to owner b // 2. Device (q, r) uses at most one panel of each owner o, namely o * 2 + send_list[o, r, q], and only where send_list[o, r, q] < 2. `send_list`: the value 2 means that requester q uses no panel of owner o.
All inputs are finite; a program needn't handle non-finite values.
Results may differ from a plain program's by a relative error of at most 0.0026.
Values may be sent and summed in bfloat16 or wider, within the bound.
A program may use at most 128 MiB of HBM per device.

v0:
```python
import math

import jax
import jax.numpy as jnp
from jax import lax
from jax.sharding import PartitionSpec as P

CONF_SLOPE = 0.5
ERR_SCALE = 1.0 / 64.0


def tile_terms(user_strip, panels, counts, users_idx, fetch_index, slot_index, slot_count):
    tile_count = counts.shape[0]
    group_size = math.gcd(tile_count, 32)
    group_count = tile_count // group_size
    side = counts.shape[-1]
    width = panels.shape[-1]

    def tile_step(totals, inputs):
        user_total, slot_total = totals
        block_counts, block_user, block_fetch, block_slot = inputs
        user_rows = user_strip[block_user]
        item_rows = panels[block_fetch]
        predicted = jnp.einsum(
            "gur,gir->gui", user_rows, item_rows, preferred_element_type=jnp.float32
        )
        amount = block_counts.astype(jnp.float32)
        confidence = 1.0 + CONF_SLOPE * amount
        preference = jnp.where(amount > 0, 1.0, 0.0).astype(jnp.float32)
        weighted_err = (confidence * (predicted - preference) * ERR_SCALE).astype(jnp.bfloat16)
        user_part = jnp.einsum(
            "gui,gir->gur", weighted_err, item_rows, preferred_element_type=jnp.float32
        )
        item_part = jnp.einsum(
            "gui,gur->gir", weighted_err, user_rows, preferred_element_type=jnp.float32
        )
        user_total = user_total.at[block_user].add(user_part)
        slot_total = slot_total.at[block_slot].add(item_part)
        return ((user_total, slot_total), None)

    start = (
        jnp.zeros((user_strip.shape[0], side, width), jnp.float32),
        jnp.zeros((slot_count, side, width), jnp.float32),
    )
    inputs = (
        counts.reshape(group_count, group_size, side, side),
        users_idx.reshape(group_count, group_size),
        fetch_index.reshape(group_count, group_size),
        slot_index.reshape(group_count, group_size),
    )
    (user_total, slot_total), _ = lax.scan(tile_step, start, inputs)
    return (user_total, slot_total)


def adagrad(factors, accum, grad):
    new_accum = accum + grad * grad
    return (factors - grad / jnp.sqrt(new_accum), new_accum)


def local(
    user_factors, user_accum, item_factors, item_accum, tile_counts, tile_user, tile_item, send_list
):
    tile_size = tile_counts.shape[-1]
    feat_width = user_factors.shape[1]
    user_strip = user_factors.astype(jnp.bfloat16).reshape(-1, tile_size, feat_width)
    owned_panels = item_factors.astype(jnp.bfloat16).reshape(-1, tile_size, feat_width)
    panels_own = owned_panels.shape[0]
    peer_count = lax.axis_size("users")
    counts = tile_counts[0, 0]
    users_idx = tile_user[0, 0]
    items_idx = tile_item[0, 0]
    send_row = send_list[0, 0]
    slot_index = items_idx // panels_own
    panels = lax.all_gather(owned_panels, "users", axis=0, tiled=True)
    user_part, slot_part = tile_terms(
        user_strip, panels, counts, users_idx, items_idx, slot_index, peer_count
    )
    returned = lax.all_to_all(
        slot_part.astype(jnp.bfloat16), "users", split_axis=0, concat_axis=0, tiled=True
    )
    selector = (send_row[None, :] == jnp.arange(panels_own, dtype=jnp.int32)[:, None]).astype(
        jnp.bfloat16
    )
    item_part = jnp.einsum("kq,qir->kir", selector, returned, preferred_element_type=jnp.float32)
    item_part = item_part.reshape(-1, feat_width)
    user_grad = lax.psum(user_part.reshape(-1, feat_width), "rep")
    new_users, new_user_accum = adagrad(user_factors, user_accum, user_grad)
    item_grad = lax.psum(item_part, "rep")
    new_items, new_item_accum = adagrad(item_factors, item_accum, item_grad)
    return (new_users, new_user_accum, new_items, new_item_accum)


def solution(mesh):
    return jax.shard_map(
        local,
        mesh=mesh,
        in_specs=(
            P("users", None),
            P("users", None),
            P("users", None),
            P("users", None),
            P("users", "rep", None, None, None),
            P("users", "rep", None),
            P("users", "rep", None),
            P("users", "rep", None),
        ),
        out_specs=(P("users", None), P("users", None), P("users", None), P("users", None)),
        check_vma=False,
    )
```

profile of v0, /device:TPU:1, one launch (start us, length us, event | category | flops | bytes accessed | tf_op | source)
XLA Modules:
  0.0 561.6 jit_solution(8553394120993238699)
XLA Ops:
  13.5 152.4 %all-gather.2.cloned.1.call-done = bf16[256,128,256]{2,1,0:T(8,128)(2,1)} async-done(((bf16[2,128,256]{2,1,0:T(8,128)(2,1)}), bf16[256,128,256]{2,1,0:T(8,128)(2,1)}) %all-gather.2.cloned.1.call-update) | async-done | bytes 16777232 | tf_op jit(solution)/shard_map/all_gather | solution.py:74
  166.0 7.8 %broadcast_in_dim.9 = f32[128,128,256]{2,1,0:T(8,128)} broadcast(f32[]{:T(128)} %constant.43.clone.1), dimensions={} | broadcast | bytes 16777220 | tf_op jit(solution)/shard_map/broadcast_in_dim | solution.py:43
  173.8 140.8 %while.12 = (s32[]{:T(128)}, f32[8,128,256]{2,1,0:T(8,128)S(1)}, f32[128,128,256]{2,1,0:T(8,128)}, s32[4,32]{1,0:T(4,128)S(1)}, bf16[4,32,128,128]{3,2,1,0:T(8,1...) while((s32[]{:T(128)}, f32[8,128,256]{2,1,0:T(8,128)S(1)}, ...), condition=%wide.region_3.4_spmd, body=%wide.region_0.3_spmd.sunk | while | flops 812124416 | bytes 71313072 | solution.py:51
  175.9 7.8 %gather_fusion.1 = bf16[32,128,256]{2,1,0:T(8,128)(2,1)} fusion(bf16[256,128,256]{2,1,0:T(8,128)(2,1)} %get-tuple-element.166, s32[1024]{0:T(1024)S(1)} %pad_clamp_fusion.5), kind=kCustom, calls=%fused_computation.1.clone.1 | custom fusion | bytes 4194432 | tf_op jit(solution)/shard_map/while/body/eval_jaxpr/gather | solution.py:23
  183.6 3.4 fusion.45
  187.0 2.8 fusion.48
  192.5 6.4 %scatter_fusion = f32[8,128,256]{2,1,0:T(8,128)S(1)} fusion(f32[8,128,256]{2,1,0:T(8,128)S(1)} %get-tuple-element.150, s32[32]{0:T(128)S(1)} %get-tuple-element.137, f32[32,128,256]{2,1,0:T(8,128)} %fusion.46), kind=kCustom, calls=%fused_computation.2.clone.1 | custom fusion | flops 1048576 | bytes 12583040 | tf_op jit(solution)/shard_map/while/body/eval_jaxpr/scatter-add | solution.py:37
  199.0 10.0 %scatter_fusion.1 = f32[128,128,256]{2,1,0:T(8,128)} fusion(f32[128,128,256]{2,1,0:T(8,128)} %get-tuple-element.151, s32[32]{0:T(128)S(1)} %fusion.47, f32[32,128,256]{2,1,0:T(8,128)} %fusion.48), kind=kCustom, calls=%fused_computation.3.clone.1 | custom fusion | flops 1048576 | bytes 12583040 | tf_op jit(solution)/shard_map/while/body/eval_jaxpr/scatter-add | solution.py:38
  211.0 7.8 %gather_fusion.1 = bf16[32,128,256]{2,1,0:T(8,128)(2,1)} fusion(bf16[256,128,256]{2,1,0:T(8,128)(2,1)} %get-tuple-element.166, s32[1024]{0:T(1024)S(1)} %pad_clamp_fusion.5), kind=kCustom, calls=%fused_computation.1.clone.1 | custom fusion | bytes 4194432 | tf_op jit(solution)/shard_map/while/body/eval_jaxpr/gather | solution.py:23
  218.7 3.4 fusion.45
  227.6 6.5 %scatter_fusion = f32[8,128,256]{2,1,0:T(8,128)S(1)} fusion(f32[8,128,256]{2,1,0:T(8,128)S(1)} %get-tuple-element.150, s32[32]{0:T(128)S(1)} %get-tuple-element.137, f32[32,128,256]{2,1,0:T(8,128)} %fusion.46), kind=kCustom, calls=%fused_computation.2.clone.1 | custom fusion | flops 1048576 | bytes 12583040 | tf_op jit(solution)/shard_map/while/body/eval_jaxpr/scatter-add | solution.py:37
  234.1 10.2 %scatter_fusion.1 = f32[128,128,256]{2,1,0:T(8,128)} fusion(f32[128,128,256]{2,1,0:T(8,128)} %get-tuple-element.151, s32[32]{0:T(128)S(1)} %fusion.47, f32[32,128,256]{2,1,0:T(8,128)} %fusion.48), kind=kCustom, calls=%fused_computation.3.clone.1 | custom fusion | flops 1048576 | bytes 12583040 | tf_op jit(solution)/shard_map/while/body/eval_jaxpr/scatter-add | solution.py:38
  246.4 7.8 %gather_fusion.1 = bf16[32,128,256]{2,1,0:T(8,128)(2,1)} fusion(bf16[256,128,256]{2,1,0:T(8,128)(2,1)} %get-tuple-element.166, s32[1024]{0:T(1024)S(1)} %pad_clamp_fusion.5), kind=kCustom, calls=%fused_computation.1.clone.1 | custom fusion | bytes 4194432 | tf_op jit(solution)/shard_map/while/body/eval_jaxpr/gather | solution.py:23
  254.1 3.4 fusion.45
  263.0 6.5 %scatter_fusion = f32[8,128,256]{2,1,0:T(8,128)S(1)} fusion(f32[8,128,256]{2,1,0:T(8,128)S(1)} %get-tuple-element.150, s32[32]{0:T(128)S(1)} %get-tuple-element.137, f32[32,128,256]{2,1,0:T(8,128)} %fusion.46), kind=kCustom, calls=%fused_computation.2.clone.1 | custom fusion | flops 1048576 | bytes 12583040 | tf_op jit(solution)/shard_map/while/body/eval_jaxpr/scatter-add | solution.py:37
  269.5 9.9 %scatter_fusion.1 = f32[128,128,256]{2,1,0:T(8,128)} fusion(f32[128,128,256]{2,1,0:T(8,128)} %get-tuple-element.151, s32[32]{0:T(128)S(1)} %fusion.47, f32[32,128,256]{2,1,0:T(8,128)} %fusion.48), kind=kCustom, calls=%fused_computation.3.clone.1 | custom fusion | flops 1048576 | bytes 12583040 | tf_op jit(solution)/shard_map/while/body/eval_jaxpr/scatter-add | solution.py:38
  281.5 7.8 %gather_fusion.1 = bf16[32,128,256]{2,1,0:T(8,128)(2,1)} fusion(bf16[256,128,256]{2,1,0:T(8,128)(2,1)} %get-tuple-element.166, s32[1024]{0:T(1024)S(1)} %pad_clamp_fusion.5), kind=kCustom, calls=%fused_computation.1.clone.1 | custom fusion | bytes 4194432 | tf_op jit(solution)/shard_map/while/body/eval_jaxpr/gather | solution.py:23
  289.2 3.4 fusion.45
  298.1 6.4 %scatter_fusion = f32[8,128,256]{2,1,0:T(8,128)S(1)} fusion(f32[8,128,256]{2,1,0:T(8,128)S(1)} %get-tuple-element.150, s32[32]{0:T(128)S(1)} %get-tuple-element.137, f32[32,128,256]{2,1,0:T(8,128)} %fusion.46), kind=kCustom, calls=%fused_computation.2.clone.1 | custom fusion | flops 1048576 | bytes 12583040 | tf_op jit(solution)/shard_map/while/body/eval_jaxpr/scatter-add | solution.py:37
  304.6 10.0 %scatter_fusion.1 = f32[128,128,256]{2,1,0:T(8,128)} fusion(f32[128,128,256]{2,1,0:T(8,128)} %get-tuple-element.151, s32[32]{0:T(128)S(1)} %fusion.47, f32[32,128,256]{2,1,0:T(8,128)} %fusion.48), kind=kCustom, calls=%fused_computation.3.clone.1 | custom fusion | flops 1048576 | bytes 12583040 | tf_op jit(solution)/shard_map/while/body/eval_jaxpr/scatter-add | solution.py:38
  314.6 6.9 %convert_element_type.19 = bf16[128,128,256]{2,1,0:T(8,128)(2,1)S(1)} convert(f32[128,128,256]{2,1,0:T(8,128)} %get-tuple-element.53) | non-fusion elementwise | flops 4194304 | bytes 25165824 | tf_op jit(solution)/shard_map/convert_element_type | solution.py:79
  321.5 192.3 %all_to_all.5 = bf16[128,128,256]{2,1,0:T(8,128)(2,1)S(1)} all-to-all(bf16[128,128,256]{2,1,0:T(8,128)(2,1)S(1)} %convert_element_type.19), channel_id=1, replica_groups=mesh['users'=128,'rep'=2] {'users'}, dimensions={0} | all-to-all | bytes 16777216 | tf_op jit(solution)/shard_map/all_to_all | solution.py:78
  513.8 4.5 fusion.11
  519.1 31.1 %all-reduce.3.cloned.1.call-done = (f32[1024,256]{1,0:T(8,128)}, f32[256,256]{1,0:T(8,128)}) async-done(((f32[1024,256]{1,0:T(8,128)}, f32[256,256]{1,0:T(8,128)}), (f32[1024,256]{1,0:T(8,128)}, f32[256,256]{1,0:T(8,128)})) %all-reduce.3.cloned.1.call-update) | async-done | bytes 1310736 | tf_op jit(solution)/shard_map/psum | solution.py:86
  (71 shorter events, 38.9 us)
Async XLA Ops:
  7.2 158.7 %all-gather.2.cloned.1.call-start = ((), (), s32[]{:S(2)}) async-start(), calls=%async_computation.1 | async-start | bytes 16908288 | tf_op jit(solution)/shard_map/all_gather | solution.py:74
  8.9 541.4 %all-reduce.3.cloned.1.call-start = ((), (), s32[]{:S(2)}) async-start(), calls=%async_computation.2 | async-start | bytes 2621440 | tf_op jit(solution)/shard_map/psum | solution.py:86
  183.6 3.4 copy-start.1
  187.0 2.8 copy-start.2
  218.7 3.4 copy-start.1
  222.2 2.8 copy-start.2
  254.1 3.4 copy-start.1
  257.5 2.8 copy-start.2
  289.2 3.4 copy-start.1
  292.7 2.8 copy-start.2
  314.6 6.9 %copy-start = (f32[8,128,256]{2,1,0:T(8,128)}, f32[8,128,256]{2,1,0:T(8,128)S(1)}, u32[]{:S(2)}) copy-start(f32[8,128,256]{2,1,0:T(8,128)S(1)} %get-tuple-element.52) | copy-start | bytes 3145732
  321.5 192.3 %copy-start.7 = (s32[1,1,128]{2,1,0:T(1,128)S(1)}, s32[1,1,128]{2,1,0:T(1,128)}, u32[]{:S(2)}) copy-start(s32[1,1,128]{2,1,0:T(1,128)} %param.17) | copy-start | bytes 1540
  513.8 36.4 %copy-start.5 = (f32[256,256]{1,0:T(8,128)S(1)}, f32[256,256]{1,0:T(8,128)}, u32[]{:S(2)}) copy-start(f32[256,256]{1,0:T(8,128)} %param.12) | copy-start | bytes 786436
  513.8 36.4 %copy-start.6 = (f32[256,256]{1,0:T(8,128)S(1)}, f32[256,256]{1,0:T(8,128)}, u32[]{:S(2)}) copy-start(f32[256,256]{1,0:T(8,128)} %param.13) | copy-start | bytes 786436
  518.3 33.7 %copy-start.3 = (f32[1024,256]{1,0:T(8,128)S(1)}, f32[1024,256]{1,0:T(8,128)}, u32[]{:S(2)}) copy-start(f32[1024,256]{1,0:T(8,128)} %param.10) | copy-start | bytes 3145732
  518.3 33.7 %copy-start.4 = (f32[1024,256]{1,0:T(8,128)S(1)}, f32[1024,256]{1,0:T(8,128)}, u32[]{:S(2)}) copy-start(f32[1024,256]{1,0:T(8,128)} %param.11) | copy-start | bytes 3145732
Sparse Core Ops, SparseCore 0:
  12.1 153.7 all-gather.1
  519.2 30.9 all-reduce.2
where the time goes:
time: 562 us
  blocking collectives  192 us (34%)
  waiting for transfers between devices  184 us (33%)
  other arithmetic  83 us (15%)
  local copies, waits for them, and re-layouts  48.4 us (9%)
  matrix products  40 us (7%)
  between operations  14.1 us (3%)
    all_to_all x1, blocking collectives, local(): lax.all_to_all(slot_part.astype(jnp.bfloat16), 'users', split_axis=0, con...  192 us
    all_gather x1, waiting for transfers between devices, local(): panels = lax.all_gather(owned_panels, 'users', axis=0, tiled=True)  152 us
    scatter-add x4, other arithmetic, tile_step(): slot_total = slot_total.at[block_slot].add(item_part)  40.1 us
    psum x1, waiting for transfers between devices, local(): user_grad = lax.psum(user_part.reshape(-1, feat_width), 'rep')  31.1 us
    gather x4, local copies, waits for them, and re-layouts, tile_step(): item_rows = panels[block_fetch]  31 us
    scatter-add x4, other arithmetic, tile_step(): user_total = user_total.at[block_user].add(user_part)  25.8 us
    dot_general x4, matrix products, tile_step(): jnp.einsum('gur,gir->gui', user_rows, item_rows, preferred_element_type=j...  13.6 us
    dot_general x4, matrix products, tile_step(): jnp.einsum('gui,gur->gir', weighted_err, user_rows, preferred_element_typ...  11.2 us
  transfers between devices with their start and end apart: 2, of which 2 were waited for; matrix products, arithmetic and copies ran while one was open for 1% of the time, Pallas kernels for 0%

commit v1 on v0

v1 whole, which is shorter than its diff:
```python
import heapq

import jax
import jax.numpy as jnp
from jax import lax
from jax.experimental import pallas as pl
from jax.experimental.pallas import tpu as pltpu
from jax.sharding import PartitionSpec as P

MESH = pl.DeviceIdType.MESH
AXES = ("z", "x", "y")
SIZE = {"z": 8, "x": 4, "y": 4}
STREAMS = (
    (slice(0, 2), 48, 16, ("x", "y", "z")),
    (slice(0, 1), 0, 48, ("y", "z", "x")),
    (slice(1, 2), 0, 48, ("x", "z", "y")),
)
HOP, RATE, PAIR_RATE = 1.7, 50e3, 500e3


def ring_steps(n):
    out = []
    for d in range(n // 2):
        for s in (1, -1):
            last = d == n // 2 - 1
            out.append((s, d, ((0,) if s == 1 else (1,)) if last else (0, 1)))
    return out


def gather_plan():
    sends = {}
    for i, (ksel, row0, rows, order) in enumerate(STREAMS):
        a, b, c = order
        unit = (ksel.stop - ksel.start) * rows * 128 * 2
        na, nb, nc = SIZE[a], SIZE[b], SIZE[c]
        p1 = [(i, 1, 0, s, d) for s, d, h in ring_steps(na)]
        for s, d, h in ring_steps(na):
            deps = [] if d == 0 else [(i, 1, 0, s, d - 1)]
            sends[(i, 1, 0, s, d)] = dict(axis=a, s=s, h=h, deps=deps, size=unit * len(h), at={a: -s * d, b: 0, c: 0})
        for s, d, h in ring_steps(nb):
            deps = p1 if d == 0 else [(i, 2, 0, s, d - 1)]
            sends[(i, 2, 0, s, d)] = dict(axis=b, s=s, h=h, deps=deps, size=unit * len(h) * na, at={a: None, b: -s * d, c: 0})
        for j in range(nb):
            off = j if j <= nb // 2 else j - nb
            if off == 0:
                line = p1
            elif abs(off) == nb // 2:
                line = [(i, 2, 0, 1, nb // 2 - 1), (i, 2, 0, -1, nb // 2 - 1)]
            else:
                line = [(i, 2, 0, -1 if off > 0 else 1, abs(off) - 1)]
            for s, d, h in ring_steps(nc):
                deps = line if d == 0 else [(i, 3, j, s, d - 1)]
                sends[(i, 3, j, s, d)] = dict(axis=c, s=s, h=h, deps=deps, size=unit * len(h) * na, at={a: None, b: off, c: -s * d})
    for i, (ksel, row0, rows, order) in enumerate(STREAMS):
        a, b, c = order
        unit = (ksel.stop - ksel.start) * rows * 256 * 2
        nb, nc = SIZE[b], SIZE[c]
        for m in range(nc):
            off = m if m <= nc // 2 else m - nc
            if off == 0:
                deps = [k for k in sends if k[0] == i and k[1] in (1, 2)]
            elif abs(off) == nc // 2:
                deps = [(i, 3, j, s, nc // 2 - 1) for j in range(nb) for s in (1, -1)]
            else:
                deps = [(i, 3, j, -1 if off > 0 else 1, abs(off) - 1) for j in range(nb)]
            sends[(i, 4, m, 0, 0)] = dict(axis="pair", s=0, h=(0, 1), deps=deps, size=unit * 128 // nc, at={a: None, b: None, c: off})
    arrive, start, free = {}, {}, {}
    pending = dict(sends)
    heap = []
    waiting = {k: set(v["deps"]) for k, v in sends.items()}
    users = {}
    for k, v in sends.items():
        for dep in v["deps"]:
            users.setdefault(dep, []).append(k)
        if not v["deps"]:
            heapq.heappush(heap, (0.0, k))
    while heap:
        t, k = heapq.heappop(heap)
        v = sends[k]
        link = (v["axis"], v["s"])
        begin = max(t, free.get(link, 0.0))
        rate = PAIR_RATE if v["axis"] == "pair" else RATE
        end = begin + v["size"] / rate
        free[link] = end
        start[k] = t
        arrive[k] = end + (0.5 if v["axis"] == "pair" else HOP)
        for q in users.get(k, ()):
            waiting[q].discard(k)
            if not waiting[q]:
                heapq.heappush(heap, (max(arrive[x] for x in sends[q]["deps"]), q))
    order = sorted(sends, key=lambda k: (start[k], k))
    return sends, order, arrive, free


def wrap(v, n):
    return lax.rem(v + 2 * n, n)


def coords():
    u = lax.axis_index("users")
    return {"z": u // 16, "x": lax.rem(u // 4, 4), "y": lax.rem(u, 4)}


def index_of(c):
    return c["z"] * 16 + c["x"] * 4 + c["y"]


def neighbour(me, axis, s):
    c = dict(me)
    c[axis] = wrap(me[axis] + s, SIZE[axis])
    return index_of(c)


def greet(me, rep):
    bar = pltpu.get_barrier_semaphore()
    for axis in AXES:
        for s in (1, -1):
            pl.semaphore_signal(bar, inc=1, device_id=(neighbour(me, axis, s), rep), device_id_type=MESH)
    pl.semaphore_signal(bar, inc=1, device_id=(index_of(me), 1 - rep), device_id_type=MESH)
    pl.semaphore_wait(bar, 7)


SENDS, ORDER, ARRIVE, FREE = gather_plan()
INDEX = {k: n for n, k in enumerate(ORDER)}


def gather_kernel(own_ref, items_ref, out_ref, other_items_ref, half, send, recv, local):
    me = coords()
    rep = lax.axis_index("rep")
    half[...] = own_ref[...].reshape(2, 128, 256).astype(jnp.bfloat16)
    lines = pl.ds(pl.multiple_of(rep * 64, 64), 64)
    keep = pltpu.make_async_copy(half.at[:, lines], out_ref.at[me["z"], me["x"], me["y"], :, lines], local)
    keep.start()
    greet(me, rep)

    def window(key):
        v = SENDS[key]
        ksel, row0, rows, order = STREAMS[key[0]]
        where = []
        for axis in AXES:
            off = v["at"][axis]
            where.append(slice(None) if off is None else wrap(me[axis] + off, SIZE[axis]))
        row = pl.ds(pl.multiple_of(rep * 64 + row0, 16), rows)
        cols = slice(None) if len(v["h"]) == 2 else pl.ds(128 * v["h"][0], 128)
        return tuple(where) + (ksel, row, cols), (ksel, row, cols)

    def copy(key):
        v = SENDS[key]
        place, mine = window(key)
        if key[1] == 4:
            target = (index_of(me), 1 - rep)
        else:
            target = (neighbour(me, v["axis"], v["s"]), rep)
        src = half.at[mine] if key[1] == 1 and not v["deps"] else out_ref.at[place]
        return pltpu.make_async_remote_copy(
            src_ref=src, dst_ref=out_ref.at[place], send_sem=send.at[INDEX[key]], recv_sem=recv.at[INDEX[key]],
            device_id=target, device_id_type=MESH,
        )

    swap = pltpu.make_async_remote_copy(
        src_ref=items_ref, dst_ref=other_items_ref, send_sem=send.at[len(ORDER)], recv_sem=recv.at[len(ORDER)],
        device_id=(index_of(me), 1 - rep), device_id_type=MESH,
    )
    swap.start()
    done = set()
    kept = False
    for key in ORDER:
        for dep in sorted(SENDS[key]["deps"], key=lambda k: ARRIVE[k]):
            if dep not in done:
                copy(dep).wait_recv()
                done.add(dep)
        if SENDS[key]["deps"] and not kept:
            keep.wait()
            kept = True
        copy(key).start()
    for key in sorted(ORDER, key=lambda k: ARRIVE[k]):
        if key not in done:
            copy(key).wait_recv()
    for key in ORDER:
        copy(key).wait_send()
    swap.wait()


def gather_panels(own, items):
    count = len(ORDER) + 1
    return pl.pallas_call(
        gather_kernel,
        out_shape=(
            jax.ShapeDtypeStruct((8, 4, 4, 2, 128, 256), jnp.bfloat16),
            jax.ShapeDtypeStruct(items.shape, items.dtype),
        ),
        in_specs=[pl.BlockSpec(memory_space=pltpu.VMEM), pl.BlockSpec(memory_space=pl.ANY)],
        out_specs=(pl.BlockSpec(memory_space=pl.ANY), pl.BlockSpec(memory_space=pl.ANY)),
        scratch_shapes=[
            pltpu.VMEM((2, 128, 256), jnp.bfloat16),
            pltpu.SemaphoreType.DMA((count,)),
            pltpu.SemaphoreType.DMA((count,)),
            pltpu.SemaphoreType.DMA,
        ],
        name="gather_panels",
        compiler_params=pltpu.CompilerParams(collective_id=0, has_side_effects=True, vmem_limit_bytes=48 * 2**20),
    )(own, items)


def reduce_steps(n):
    out = []
    for q in range(n // 2):
        for s in (1, -1):
            out.append((s, q, n // 2 - q, ((0,) if s == 1 else (1,)) if q == 0 else (0, 1)))
    return out


def far_first(n):
    out = [n // 2]
    for d in range(n // 2 - 1, 0, -1):
        out += [d, -d]
    return out + [0]


def reduce_plan():
    tasks = {}
    zs = far_first(8)
    for n, off in enumerate(zs):
        tasks[("pair", off)] = dict(kind="pair", deps=[], size=16 * 64 * 256 * 2, rank=n)
    allz = [("pair", off) for off in zs]
    for i, (ksel, row0, rows, order) in enumerate(STREAMS):
        a, b, c = order
        na, nb, nc = SIZE[a], SIZE[b], SIZE[c]
        unit = (ksel.stop - ksel.start) * rows * 128 * 2
        for rank, j in enumerate(far_first(nb)):
            def shares(dist_c):
                if b == "z":
                    return [("pair", j if j != -(nb // 2) else nb // 2)]
                if c == "z":
                    return [("pair", dist_c)]
                return allz
            for s, q, e, h in reduce_steps(nc):
                at = s * e
                if at == -(nc // 2):
                    at = nc // 2
                deps = shares(at) + ([("send", i, 1, j, s, q - 1)] if q else [])
                tasks[("send", i, 1, j, s, q)] = dict(kind="send", axis=c, s=s, h=h, deps=deps, size=unit * len(h) * na, rank=rank, e=s * e)
            last = nc // 2 - 1
            tasks[("sum", i, 1, j)] = dict(kind="sum", deps=shares(0) + [("send", i, 1, j, s, last) for s in (1, -1)], size=unit * 2 * na, rank=rank)
        for s, q, e, h in reduce_steps(nb):
            line = s * e if s * e != -(nb // 2) else nb // 2
            deps = [("sum", i, 1, line)] + ([("send", i, 2, 0, s, q - 1)] if q else [])
            tasks[("send", i, 2, 0, s, q)] = dict(kind="send", axis=b, s=s, h=h, deps=deps, size=unit * len(h) * na, rank=-5, e=line)
        tasks[("sum", i, 2)] = dict(kind="sum", deps=[("sum", i, 1, 0)] + [("send", i, 2, 0, s, nb // 2 - 1) for s in (1, -1)], size=unit * 2 * na, rank=-5)
        for s, q, e, h in reduce_steps(na):
            deps = [("sum", i, 2)] + ([("send", i, 3, 0, s, q - 1)] if q else [])
            tasks[("send", i, 3, 0, s, q)] = dict(kind="send", axis=a, s=s, h=h, deps=deps, size=2 * unit * len(h), rank=-9, e=s * e)
        tasks[("sum", i, 3)] = dict(kind="sum", deps=[("sum", i, 2)] + [("send", i, 3, 0, s, na // 2 - 1) for s in (1, -1)], size=unit * 2, rank=-9)
    done_at, free, order = {}, {}, []
    left = dict(tasks)
    for k in [k for k in left if k[0] == "pair"]:
        v = left.pop(k)
        begin = free.get("pair", 0.0)
        free["pair"] = begin + v["size"] / PAIR_RATE
        done_at[k] = free["pair"] + 0.7
        order.append(k)
    now = 0.0
    while left:
        best = None
        for k, v in left.items():
            if all(d in done_at for d in v["deps"]):
                ready = max([done_at[d] for d in v["deps"]])
                link = free.get((v["axis"], v["s"]), 0.0) if v["kind"] == "send" else 0.0
                begin = max(ready, now)
                score = (max(begin, link if link > begin + 2.0 else 0.0), v["rank"], -k[-1] if v["kind"] == "send" else -9)
                if best is None or score < best[0]:
                    best = (score, k, begin)
        _, k, begin = best
        v = left.pop(k)
        now = begin + 0.05 + v["size"] / 900e3
        if v["kind"] == "send":
            link = (v["axis"], v["s"])
            free[link] = max(now, free.get(link, 0.0)) + v["size"] / RATE
            done_at[k] = free[link] + HOP
        else:
            done_at[k] = now
        order.append(k)
    return tasks, order, done_at, free


TASKS, TASK_ORDER, DONE_AT, LINKS = reduce_plan()
SEND_INDEX = {k: n for n, k in enumerate([k for k in TASK_ORDER if k[0] != "sum"])}


def dims(i):
    ksel, row0, rows, order = STREAMS[i]
    return ksel.stop - ksel.start, rows, tuple(SIZE[x] for x in order)


def reduce_kernel(slots_ref, used_ref, user_ref, user_out, grad_out, mine, other, *rest):
    bufs = [dict(zip(("s1", "r1", "l1", "s2", "r2", "l2", "s3", "r3"), rest[8 * i: 8 * i + 8])) for i in range(3)]
    total, send, recv, load, last = rest[24:]
    me = coords()
    rep = lax.axis_index("rep")
    row_mine = pl.multiple_of(rep * 64, 64)
    row_other = pl.multiple_of((1 - rep) * 64, 64)
    zof = {off: wrap(me["z"] + off, 8) for off in range(-4, 5)}
    loads = {}
    for n, off in enumerate(far_first(8)):
        loads[off] = pltpu.make_async_copy(slots_ref.at[zof[off], :, :, pl.ds(row_mine, 64), :], mine.at[zof[off]], load.at[n])
        loads[off].start()
    greet(me, rep)
    pair = (index_of(me), 1 - rep)

    def remote(key):
        if key[0] == "pair":
            z = zof[key[1]]
            return pltpu.make_async_remote_copy(
                src_ref=slots_ref.at[z, :, :, pl.ds(row_other, 64), :], dst_ref=other.at[z],
                send_sem=send.at[SEND_INDEX[key]], recv_sem=recv.at[SEND_INDEX[key]], device_id=pair, device_id_type=MESH)
        _, i, phase, j, s, q = key
        v = TASKS[key]
        nb = dims(i)[2][1]
        cols = pl.ds(0, 256) if len(v["h"]) == 2 else pl.ds(128 * v["h"][0], 128)
        side = 0 if s == 1 else 1
        at = (j % nb, side, q) if phase == 1 else (side, q)
        tail = (slice(None),) * (2 if phase == 3 else 3) + (cols,)
        return pltpu.make_async_remote_copy(
            src_ref=bufs[i]["s%d" % phase].at[at + tail], dst_ref=bufs[i]["r%d" % phase].at[at + tail],
            send_sem=send.at[SEND_INDEX[key]], recv_sem=recv.at[SEND_INDEX[key]],
            device_id=(neighbour(me, v["axis"], s), rep), device_id_type=MESH)

    def share(i, offs, n, cols):
        ksel, row0, rows, order = STREAMS[i]
        a, b, c = order
        where = {b: wrap(me[b] + offs[0], SIZE[b]), c: wrap(me[c] + offs[1], SIZE[c]), a: n}
        owner = index_of(where)
        place = (where["z"], where["x"], where["y"], pl.ds(row0, rows), cols)
        x = mine[place].astype(jnp.float32)
        y = other[place].astype(jnp.float32)
        out = []
        for k in range(ksel.start, ksel.stop):
            ux = used_ref[0, owner * 2 + k] > 0
            uy = used_ref[1, owner * 2 + k] > 0
            out.append(jnp.where(ux, x, 0.0) + jnp.where(uy, y, 0.0))
        return out

    def work(key):
        v = TASKS[key]
        i = key[1]
        kk, rows, (na, nb, nc) = dims(i)
        buf = bufs[i]
        if key[0] == "send":
            _, i, phase, j, s, q = key
            side = 0 if s == 1 else 1
            for h in ((0, 1) if (q == 1) else (None,)):
                cols = pl.ds(128 * h, 128) if h is not None else (pl.ds(0, 256) if len(v["h"]) == 2 else pl.ds(128 * v["h"][0], 128))
                got = q >= 2 or (q == 1 and h == side)

                def body(n, _, cols=cols, got=got):
                    if phase == 1:
                        parts = share(i, (j, v["e"]), n, cols)
                    elif phase == 2:
                        parts = [buf["l1"][v["e"] % nb, n, k, :, cols] for k in range(kk)]
                    for k in range(kk):
                        x = parts[k]
                        if phase == 1:
                            if got:
                                x = x + buf["r1"][j % nb, side, q - 1, n, k, :, cols].astype(jnp.float32)
                            buf["s1"][j % nb, side, q, n, k, :, cols] = x.astype(jnp.bfloat16)
                        else:
                            if got:
                                x = x + buf["r2"][side, q - 1, n, k, :, cols].astype(jnp.float32)
                            buf["s2"][side, q, n, k, :, cols] = x.astype(jnp.bfloat16)
                    return 0

                if phase == 3:
                    n = wrap(me[STREAMS[i][3][0]] + v["e"], na)
                    for k in range(kk):
                        x = buf["l2"][n, k, :, cols]
                        if got:
                            x = x + buf["r3"][side, q - 1, k, :, cols]
                        buf["s3"][side, q, k, :, cols] = x
                else:
                    lax.fori_loop(0, na, body, 0)
            return
        phase = key[2]
        end = {1: nc, 2: nb, 3: na}[phase] // 2 - 1
        full = pl.ds(0, 256)
        if phase == 1:
            j = key[3]

            def body(n, _):
                parts = share(i, (j, 0), n, full)
                for k in range(kk):
                    x = parts[k]
                    for side in range(2):
                        x = x + buf["r1"][j % nb, side, end, n, k].astype(jnp.float32)
                    buf["l1"][j % nb, n, k] = x
                return 0

            lax.fori_loop(0, na, body, 0)
        elif phase == 2:

            def body(n, _):
                for k in range(kk):
                    x = buf["l1"][0, n, k]
                    for side in range(2):
                        x = x + buf["r2"][side, end, n, k].astype(jnp.float32)
                    buf["l2"][n, k] = x
                return 0

            lax.fori_loop(0, na, body, 0)
        else:
            ksel, row0, rows, order = STREAMS[i]
            n = me[order[0]]
            for k in range(kk):
                x = buf["l2"][n, k]
                for side in range(2):
                    x = x + buf["r3"][side, end, k]
                total[ksel.start + k, pl.ds(row0, rows), :] = x

    swap = pltpu.make_async_remote_copy(
        src_ref=user_ref, dst_ref=user_out, send_sem=last.at[0], recv_sem=last.at[1], device_id=pair, device_id_type=MESH)
    done = set()
    swapped = False
    for key in TASK_ORDER:
        if key[0] == "pair":
            remote(key).start()
            continue
        if not swapped:
            swap.start()
            swapped = True
        for dep in sorted(TASKS[key]["deps"], key=lambda k: DONE_AT[k]):
            if dep[0] == "sum" or dep in done:
                continue
            if dep[0] == "pair":
                loads[dep[1]].wait()
            remote(dep).wait_recv()
            done.add(dep)
        work(key)
        if key[0] == "send":
            remote(key).start()
    keep = pltpu.make_async_copy(total, grad_out.at[:, pl.ds(row_mine, 64), :], last.at[2])
    give = pltpu.make_async_remote_copy(
        src_ref=total, dst_ref=grad_out.at[:, pl.ds(row_mine, 64), :], send_sem=last.at[3], recv_sem=last.at[4],
        device_id=pair, device_id_type=MESH)
    keep.start()
    give.start()
    for key in SEND_INDEX:
        if key not in done:
            if key[0] == "pair":
                loads[key[1]].wait()
            remote(key).wait_recv()
        remote(key).wait_send()
    swap.wait()
    keep.wait()
    give.wait()


def reduce_parts(slots, used, user_part):
    scratch = [pltpu.VMEM((8, 4, 4, 64, 256), jnp.bfloat16)] * 2
    for i in range(3):
        kk, rows, (na, nb, nc) = dims(i)
        unit = (kk, rows, 256)
        scratch += [pltpu.VMEM((nb, 2, nc // 2, na) + unit, jnp.bfloat16)] * 2
        scratch += [pltpu.VMEM((nb, na) + unit, jnp.float32)]
        scratch += [pltpu.VMEM((2, nb // 2, na) + unit, jnp.bfloat16)] * 2
        scratch += [pltpu.VMEM((na,) + unit, jnp.float32)]
        scratch += [pltpu.VMEM((2, na // 2) + unit, jnp.float32)] * 2
    count = len(SEND_INDEX)
    scratch += [
        pltpu.VMEM((2, 64, 256), jnp.float32),
        pltpu.SemaphoreType.DMA((count,)), pltpu.SemaphoreType.DMA((count,)),
        pltpu.SemaphoreType.DMA((8,)), pltpu.SemaphoreType.DMA((5,)),
    ]
    anywhere = pl.BlockSpec(memory_space=pl.ANY)
    return pl.pallas_call(
        reduce_kernel,
        out_shape=(
            jax.ShapeDtypeStruct(user_part.shape, jnp.float32),
            jax.ShapeDtypeStruct((2, 128, 256), jnp.float32),
        ),
        in_specs=[anywhere, pl.BlockSpec(memory_space=pltpu.SMEM), anywhere],
        out_specs=(anywhere, anywhere),
        scratch_shapes=scratch,
        name="reduce_parts",
        compiler_params=pltpu.CompilerParams(collective_id=1, has_side_effects=True, vmem_limit_bytes=56 * 2**20),
    )(slots.reshape(8, 4, 4, 128, 256), used, user_part)


GROUP, RING = 4, 16


def tiles_kernel(keys_ref, panels_ref, counts_ref, users_ref, slots_out, user_out, half, vbuf, cbuf, acc, stage, vsem, csem, ssem):
    tiles = counts_ref.shape[0]

    def key(i):
        return keys_ref[jnp.clip(i, 0, tiles - 1)]

    def owner(i):
        return lax.shift_right_logical(key(i), 11)

    def fetch(i):
        k = key(i)
        slot = lax.rem(i, RING)
        item = lax.shift_right_logical(k, 10)
        tile = lax.rem(lax.shift_right_logical(k, 3), 128)
        return (
            pltpu.make_async_copy(panels_ref.at[item], vbuf.at[slot], vsem.at[slot]),
            pltpu.make_async_copy(counts_ref.at[tile], cbuf.at[slot], csem.at[slot]),
        )

    def put(i):
        slot = lax.rem(i, RING)
        return pltpu.make_async_copy(stage.at[slot], slots_out.at[owner(i)], ssem.at[slot])

    def is_last(i):
        return (i == tiles - 1) | (owner(i) != owner(i + 1))

    def start(i, _):
        for c in fetch(i):
            c.start()
        return 0

    lax.fori_loop(0, RING, start, 0)
    half[...] = users_ref[...].astype(jnp.bfloat16)
    user_out[...] = jnp.zeros_like(user_out)
    acc[...] = jnp.zeros_like(acc)

    def group(g, _):
        base = g * GROUP
        for n in range(GROUP):
            i = base + n
            for c in fetch(i):
                c.wait()

            @pl.when((i >= RING) & is_last(i - RING))
            def _():
                put(i - RING).wait()

        errs = []
        for n in range(GROUP):
            i = base + n
            slot = lax.rem(i, RING)
            block = lax.rem(key(i), 8)
            u = half[block]
            v = vbuf[slot]
            predicted = lax.dot_general(u, v, (((1,), (1,)), ((), ())), preferred_element_type=jnp.float32)
            amount = cbuf[slot].astype(jnp.float32)
            weight = amount * (0.5 / 64.0) + 1.0 / 64.0
            errs.append((weight * (predicted - jnp.where(amount > 0, 1.0, 0.0))).astype(jnp.bfloat16))
        for n in range(GROUP):
            i = base + n
            slot = lax.rem(i, RING)
            block = lax.rem(key(i), 8)
            first = (i == 0) | (owner(i) != owner(i - 1))
            item_part = lax.dot_general(errs[n], half[block], (((0,), (0,)), ((), ())), preferred_element_type=jnp.float32)
            total = jnp.where(first, 0.0, acc[...]) + item_part
            acc[...] = total
            stage[slot] = total.astype(jnp.bfloat16)
            user_out[block] += jnp.dot(errs[n], vbuf[slot], preferred_element_type=jnp.float32)
        for n in range(GROUP):
            i = base + n

            @pl.when(is_last(i))
            def _():
                put(i).start()

            @pl.when(i + RING < tiles)
            def _():
                for c in fetch(i + RING):
                    c.start()

        return 0

    lax.fori_loop(0, tiles // GROUP, group, 0)

    def finish(n, _):
        i = tiles - RING + n

        @pl.when(is_last(i))
        def _():
            put(i).wait()

        return 0

    lax.fori_loop(0, RING, finish, 0)


def tile_parts(keys, panels, counts, users):
    anywhere = pl.BlockSpec(memory_space=pl.ANY)
    whole = pl.BlockSpec(memory_space=pltpu.VMEM)
    return pl.pallas_call(
        tiles_kernel,
        out_shape=(
            jax.ShapeDtypeStruct((128, 128, 256), jnp.bfloat16),
            jax.ShapeDtypeStruct((8, 128, 256), jnp.float32),
        ),
        in_specs=[pl.BlockSpec(memory_space=pltpu.SMEM), anywhere, anywhere, whole],
        out_specs=(anywhere, whole),
        scratch_shapes=[
            pltpu.VMEM((8, 128, 256), jnp.bfloat16),
            pltpu.VMEM((RING, 128, 256), jnp.bfloat16),
            pltpu.VMEM((RING, 128, 128), jnp.bfloat16),
            pltpu.VMEM((128, 256), jnp.float32),
            pltpu.VMEM((RING, 128, 256), jnp.bfloat16),
            pltpu.SemaphoreType.DMA((RING,)),
            pltpu.SemaphoreType.DMA((RING,)),
            pltpu.SemaphoreType.DMA((RING,)),
        ],
        name="tile_parts",
        compiler_params=pltpu.CompilerParams(vmem_limit_bytes=40 * 2**20),
        cost_estimate=pl.CostEstimate(flops=128 * 6 * 128 * 128 * 256, bytes_accessed=26 * 2**20, transcendentals=0),
    )(keys, panels, counts, users)


def sorted_keys(items, blocks):
    key = (items * 128 + jnp.arange(items.shape[0], dtype=jnp.int32)) * 8 + blocks
    rank = jnp.sum((key[None, :] < key[:, None]).astype(jnp.int32), axis=1)
    place = jnp.arange(items.shape[0], dtype=jnp.int32)
    return jnp.sum(jnp.where(rank[None, :] == place[:, None], key[None, :], 0), axis=1)


def adagrad(factors, accum, grad):
    new_accum = accum + grad * grad
    return factors - grad / jnp.sqrt(new_accum), new_accum


def local(user_factors, user_accum, item_factors, item_accum, tile_counts, tile_user, tile_item, send_list):
    counts = tile_counts[0, 0]
    items = tile_item[0, 0]
    keys = sorted_keys(items, tile_user[0, 0])
    panels, other_items = gather_panels(item_factors, items[None, :])
    both = jnp.stack([items, other_items[0]])
    used = jnp.any(both[:, :, None] == jnp.arange(256, dtype=jnp.int32), axis=1).astype(jnp.int32)
    slots, user_part = tile_parts(keys, panels.reshape(256, 128, 256), counts, user_factors.reshape(8, 128, 256))
    other_user, item_grad = reduce_parts(slots, used, user_part.reshape(1024, 256))
    user_grad = user_part.reshape(1024, 256) + other_user
    new_users, new_user_accum = adagrad(user_factors, user_accum, user_grad)
    new_items, new_item_accum = adagrad(item_factors, item_accum, item_grad.reshape(256, 256))
    return new_users, new_user_accum, new_items, new_item_accum


def solution(mesh):
    rows = P("users", None)
    return jax.shard_map(
        local,
        mesh=mesh,
        in_specs=(rows, rows, rows, rows, P("users", "rep", None, None, None), P("users", "rep", None), P("users", "rep", None), P("users", "rep", None)),
        out_specs=(rows, rows, rows, rows),
        check_vma=False,
    )
```

time: 562 us -> 162 us (0.29)
  blocking collectives: 192 us -> 0 us
  waiting for transfers between devices: 184 us -> 0 us
  Pallas kernels: 0 us -> 148 us
  other arithmetic: 83 us -> 6.25 us
  local copies, waits for them, and re-layouts: 48.4 us -> 6 us
  matrix products: 40 us -> 0 us
  between operations: 14.1 us -> 0.74 us
    all_to_all x1 -> x0, blocking collectives: 192 us -> none  [local(): lax.all_to_all(slot_part.astype(jnp.bfloat16), 'users', split_axis=0, con...]
    all_gather x1 -> x0, waiting for transfers between devices: 152 us -> none  [local(): panels = lax.all_gather(owned_panels, 'users', axis=0, tiled=True)]
    pallas_call x0 -> x3, Pallas kernels: none -> 148 us  [the longest x1 66 us: gather_panels(): pl.pallas_call(gather_kernel, out_shape=(jax.ShapeDtypeStruct((8, 4, 4, 2...]
    scatter-add x8 -> x0, other arithmetic: 65.9 us -> none  [the longest x4 40.1 us: tile_step(): slot_total = slot_total.at[block_slot].add(item_part)]
    dot_general x13 -> x0, matrix products: 40 us -> none  [the longest x4 13.6 us: tile_step(): jnp.einsum('gur,gir->gui', user_rows, item_rows, preferred_element_type=j...]
    gather x8 -> x0, local copies, waits for them, and re-layouts: 39.1 us -> none  [the longest x4 31 us: tile_step(): item_rows = panels[block_fetch]]
    psum x1 -> x0, waiting for transfers between devices: 31.1 us -> none  [local(): user_grad = lax.psum(user_part.reshape(-1, feat_width), 'rep')]
    convert_element_type x3 -> x1, other arithmetic: 9.77 us -> 0.58 us  [local(): jnp.any(both[:, :, None] == jnp.arange(256, dtype=jnp.int32), axis=1)]
  transfers between devices with their start and end apart: 2 -> 0, of which waited for: 2 -> 0; matrix products, arithmetic and copies ran while one was open for 1% -> 0% of each run, Pallas kernels for 0% -> 0%
where the time goes in v1:
time: 162 us; the launch traced here: 161 us
  Pallas kernels  148 us (91%)
  other arithmetic  6.25 us (4%)
  local copies, waits for them, and re-layouts  6 us (4%)
    pallas_call x1, Pallas kernels, gather_panels(): pl.pallas_call(gather_kernel, out_shape=(jax.ShapeDtypeStruct((8, 4, 4, 2...  66 us
    pallas_call x1, Pallas kernels, reduce_parts(): pl.pallas_call(reduce_kernel, out_shape=(jax.ShapeDtypeStruct(user_part.s...  54.8 us
    pallas_call x1, Pallas kernels, tile_parts(): pl.pallas_call(tiles_kernel, out_shape=(jax.ShapeDtypeStruct((128, 128, 2...  27.6 us
    unnamed x20, local copies, waits for them, and re-layouts  6 us
    sub x2, other arithmetic, adagrad(): return (factors - grad / jnp.sqrt(new_accum), new_accum)  4.58 us

profile of v1, /device:TPU:1, one launch (start us, length us, event | category | flops | bytes accessed | tf_op | source)
XLA Modules:
  0.0 161.4 jit_solution(6833685639949880071)
XLA Ops:
  0.6 0.7 bitcast_add_fusion
  1.3 0.2 convert_reduce_fusion
  1.5 0.1 select_reduce_fusion.keys_ref
  1.6 0.0 copy-start.5
  1.6 0.9 copy-done.5
  2.6 0.7 copy-done.7
  3.2 66.0 %gather_panels.1 = (bf16[8,4,4,2,128,256]{5,4,3,2,1,0:T(8,128)(2,1)}, s32[1,128]{1,0:T(1,128)S(1)}) custom-call(f32[256,256]{1,0:T(8,128)S(1)} %copy-done.5, s32[1,128]{1,0:T(1,128)S(1)} %bitcast.31), custom_call_target="tpu_custom_call" | custom-call | tf_op jit(solution)/shard_map/gather_panels/pallas_call | solution.py:186
  69.3 0.0 copy-start
  69.3 1.2 copy-done
  70.5 2.2 %copy-done.4 = bf16[1,1,128,128,128]{4,3,2,1,0:T(8,128)(2,1)S(1)} copy-done((bf16[1,1,128,128,128]{4,3,2,1,0:T(8,128)(2,1)S(1)}, bf16[1,1,128,128,128]{4,3,2,1,0:T(8,128)(2,1)}, u32[]{:S(2)}) %copy-start.4) | copy-done | bytes 4194328
  72.7 27.6 %tile_parts.1 = (bf16[128,128,256]{2,1,0:T(8,128)(2,1)}, f32[8,128,256]{2,1,0:T(8,128)S(1)}) custom-call(s32[128]{0:T(128)S(1)} %select_reduce_fusion.keys_ref, bf16[256,128,256]{2,1,0:T(8,128)(2,1)} %bitcast.33, bf16[128,128,128]{2,1,0:T(8,128)(2,1)S(1)} %bitcast.30, f32[8,128,256]{2,1,0:T(8,128)S(1)} %bitcast.28), custom_call_target="tpu_custom_call" | custom-call | flops 3221225472 | bytes 27262976 | tf_op jit(solution)/shard_map/tile_parts/pallas_call | solution.py:589
  100.3 0.0 copy-start.2
  100.3 1.0 copy-done.2
  101.3 0.0 copy-start.3
  101.3 0.1 fusion.2
  101.4 0.6 convert_element_type.7.used_ref
  102.0 54.8 %reduce_parts.1 = (f32[1024,256]{1,0:T(8,128)}, f32[2,128,256]{2,1,0:T(8,128)}) custom-call(bf16[8,4,4,128,256]{4,3,2,1,0:T(8,128)(2,1)} %bitcast.34, s32[2,256]{1,0:T(2,128)} %convert_element_type.7.used_ref, f32[1024,256]{1,0:T(8,128)} %bitcast.29), custom_call_target="tpu_custom_call" | custom-call | tf_op jit(solution)/shard_map/reduce_parts/pallas_call | solution.py:473
  156.8 0.0 copy-done.1
  156.8 0.0 copy-done.8
  156.8 0.0 copy-done.3
  156.9 2.8 %multiply_subtract_fusion = (f32[1024,256]{1,0:T(8,128)}, f32[1024,256]{1,0:T(8,128)}) fusion(f32[1024,256]{1,0:T(8,128)S(1)} %copy-done.1, f32[1024,256]{1,0:T(8,128)} %get-tuple-element.14, f32[8,128,256]{2,1,0:T(8,128)S(1)} %copy-done.3, f32[1024,256]{1,0:T(8,128)S(1)} %copy-done.8), kind=kLoop, calls=%fused_computation | loop fusion | flops 1310720 | bytes 6291456 | tf_op jit(solution)/shard_map/sub | solution.py:622
  159.6 0.0 copy-done.6
  159.6 0.0 copy-done.9
  159.6 1.8 %fusion.1 = (f32[256,256]{1,0:T(8,128)}, f32[256,256]{1,0:T(8,128)}) fusion(f32[256,256]{1,0:T(8,128)S(1)} %copy-done.6, f32[2,128,256]{2,1,0:T(8,128)} %get-tuple-element.15, f32[256,256]{1,0:T(8,128)S(1)} %copy-done.9), kind=kLoop, calls=%fused_computation.5 | loop fusion | flops 262144 | bytes 1310720 | tf_op jit(solution)/shard_map/sub | solution.py:622
  (7 shorter events, 0.0 us)
Async XLA Ops:
  1.6 1.0 copy-start.5
  2.6 0.7 copy-start.7
  69.3 1.2 copy-start
  70.5 2.2 %copy-start.4 = (bf16[1,1,128,128,128]{4,3,2,1,0:T(8,128)(2,1)S(1)}, bf16[1,1,128,128,128]{4,3,2,1,0:T(8,128)(2,1)}, u32[]{:S(2)}) copy-start(bf16[1,1,128,128,128]{4,3,2,1,0:T(8,128)(2,1)} %param.12) | copy-start | bytes 12582916
  100.3 1.0 copy-start.2
  101.3 55.6 %copy-start.1 = (f32[1024,256]{1,0:T(8,128)S(1)}, f32[1024,256]{1,0:T(8,128)}, u32[]{:S(2)}) copy-start(f32[1024,256]{1,0:T(8,128)} %param.8) | copy-start | bytes 3145732
  101.3 55.6 %copy-start.8 = (f32[1024,256]{1,0:T(8,128)S(1)}, f32[1024,256]{1,0:T(8,128)}, u32[]{:S(2)}) copy-start(f32[1024,256]{1,0:T(8,128)} %param.9) | copy-start | bytes 3145732
  101.3 58.4 %copy-start.6 = (f32[256,256]{1,0:T(8,128)S(1)}, f32[256,256]{1,0:T(8,128)}, u32[]{:S(2)}) copy-start(f32[256,256]{1,0:T(8,128)} %own_ref.1) | copy-start | bytes 786436
  101.3 58.4 %copy-start.9 = (f32[256,256]{1,0:T(8,128)S(1)}, f32[256,256]{1,0:T(8,128)}, u32[]{:S(2)}) copy-start(f32[256,256]{1,0:T(8,128)} %param.11) | copy-start | bytes 786436
  101.3 55.6 %copy-start.3 = (f32[8,128,256]{2,1,0:T(8,128)S(1)}, f32[8,128,256]{2,1,0:T(8,128)}, u32[]{:S(2)}) copy-start(f32[8,128,256]{2,1,0:T(8,128)} %copy-done.2) | copy-start | bytes 3145732

commit v2 on v1

--- a/solution.py
+++ b/solution.py
@@ -1,3 +1,4 @@
+import functools
 import heapq
 
 import jax
@@ -10,12 +11,16 @@
 MESH = pl.DeviceIdType.MESH
 AXES = ("z", "x", "y")
 SIZE = {"z": 8, "x": 4, "y": 4}
-STREAMS = (
+GATHER_STREAMS = (
     (slice(0, 2), 48, 16, ("x", "y", "z")),
     (slice(0, 1), 0, 48, ("y", "z", "x")),
     (slice(1, 2), 0, 48, ("x", "z", "y")),
 )
-HOP, RATE, PAIR_RATE = 1.7, 50e3, 500e3
+RATE, PAIR_RATE, HOP, PAIR_HOP, ISSUE, AHEAD = 45e3, 500e3, 1.7, 0.8, 0.07, 2.5
+
+
+def signed(j, n):
+    return j if j <= n // 2 else j - n
 
 
 def ring_steps(n):
@@ -27,69 +32,96 @@
     return out
 
 
-def gather_plan():
+def gather_sends(streams):
     sends = {}
-    for i, (ksel, row0, rows, order) in enumerate(STREAMS):
+    for i, (panels, row0, rows, order) in enumerate(streams):
         a, b, c = order
-        unit = (ksel.stop - ksel.start) * rows * 128 * 2
+        unit = (panels.stop - panels.start) * rows * 128 * 2
         na, nb, nc = SIZE[a], SIZE[b], SIZE[c]
-        p1 = [(i, 1, 0, s, d) for s, d, h in ring_steps(na)]
-        for s, d, h in ring_steps(na):
-            deps = [] if d == 0 else [(i, 1, 0, s, d - 1)]
-            sends[(i, 1, 0, s, d)] = dict(axis=a, s=s, h=h, deps=deps, size=unit * len(h), at={a: -s * d, b: 0, c: 0})
+        first = [(s, d, (0, 1)) for s, d, h in ring_steps(na) if s == 1 or d < na // 2 - 1]
+        near = [(i, 1, 0, s, d) for s, d, h in first]
+
+        def add(key, axis, h, deps, size, at):
+            sends[key] = dict(axis=axis, s=key[3], h=h, deps=deps, size=size, at=at)
+
+        for s, d, h in first:
+            add((i, 1, 0, s, d), a, h, [] if d == 0 else [(i, 1, 0, s, d - 1)], unit * 2, {a: -s * d, b: 0, c: 0})
         for s, d, h in ring_steps(nb):
-            deps = p1 if d == 0 else [(i, 2, 0, s, d - 1)]
-            sends[(i, 2, 0, s, d)] = dict(axis=b, s=s, h=h, deps=deps, size=unit * len(h) * na, at={a: None, b: -s * d, c: 0})
+            deps = near if d == 0 else [(i, 2, 0, s, d - 1)]
+            add((i, 2, 0, s, d), b, h, deps, unit * len(h) * na, {a: None, b: -s * d, c: 0})
         for j in range(nb):
-            off = j if j <= nb // 2 else j - nb
+            off = signed(j, nb)
             if off == 0:
-                line = p1
-            elif abs(off) == nb // 2:
-                line = [(i, 2, 0, 1, nb // 2 - 1), (i, 2, 0, -1, nb // 2 - 1)]
+                line = near
+            elif off == nb // 2:
+                line = [(i, 2, 0, s, nb // 2 - 1) for s in (1, -1)]
             else:
                 line = [(i, 2, 0, -1 if off > 0 else 1, abs(off) - 1)]
             for s, d, h in ring_steps(nc):
                 deps = line if d == 0 else [(i, 3, j, s, d - 1)]
-                sends[(i, 3, j, s, d)] = dict(axis=c, s=s, h=h, deps=deps, size=unit * len(h) * na, at={a: None, b: off, c: -s * d})
-    for i, (ksel, row0, rows, order) in enumerate(STREAMS):
-        a, b, c = order
-        unit = (ksel.stop - ksel.start) * rows * 256 * 2
-        nb, nc = SIZE[b], SIZE[c]
-        for m in range(nc):
-            off = m if m <= nc // 2 else m - nc
-            if off == 0:
-                deps = [k for k in sends if k[0] == i and k[1] in (1, 2)]
-            elif abs(off) == nc // 2:
-                deps = [(i, 3, j, s, nc // 2 - 1) for j in range(nb) for s in (1, -1)]
-            else:
-                deps = [(i, 3, j, -1 if off > 0 else 1, abs(off) - 1) for j in range(nb)]
-            sends[(i, 4, m, 0, 0)] = dict(axis="pair", s=0, h=(0, 1), deps=deps, size=unit * 128 // nc, at={a: None, b: None, c: off})
-    arrive, start, free = {}, {}, {}
-    pending = dict(sends)
-    heap = []
-    waiting = {k: set(v["deps"]) for k, v in sends.items()}
-    users = {}
+                add((i, 3, j, s, d), c, h, deps, unit * len(h) * na, {a: None, b: off, c: -s * d})
+            deps = line + [(i, 3, j, s, d) for s, d, h in ring_steps(nc)]
+            add((i, 4, j, 0, 0), "pair", (0, 1), deps, unit * 2 * na * nc, {a: None, b: off, c: None})
+    return sends
+
+
+def timeline(sends, rank):
+    users, waiting, ready, begin, arrive, queue, busy, events = {}, {}, {}, {}, {}, {}, {}, []
+    core, count = 0.0, 0
     for k, v in sends.items():
+        waiting[k] = len(v["deps"])
         for dep in v["deps"]:
             users.setdefault(dep, []).append(k)
         if not v["deps"]:
-            heapq.heappush(heap, (0.0, k))
-    while heap:
-        t, k = heapq.heappop(heap)
-        v = sends[k]
-        link = (v["axis"], v["s"])
-        begin = max(t, free.get(link, 0.0))
-        rate = PAIR_RATE if v["axis"] == "pair" else RATE
-        end = begin + v["size"] / rate
-        free[link] = end
-        start[k] = t
-        arrive[k] = end + (0.5 if v["axis"] == "pair" else HOP)
-        for q in users.get(k, ()):
-            waiting[q].discard(k)
-            if not waiting[q]:
-                heapq.heappush(heap, (max(arrive[x] for x in sends[q]["deps"]), q))
-    order = sorted(sends, key=lambda k: (start[k], k))
-    return sends, order, arrive, free
+            ready[k] = 0.0
+            heapq.heappush(events, (0.0, count, "ready", k))
+            count += 1
+    while events:
+        now = events[0][0]
+        touched = []
+        while events and events[0][0] <= now + 1e-9:
+            _, _, what, k = heapq.heappop(events)
+            if what == "arrive":
+                for q in users.get(k, ()):
+                    waiting[q] -= 1
+                    if waiting[q] == 0:
+                        core = max(core, now) + ISSUE + sends[q].get("work", 0.0)
+                        ready[q] = core
+                        heapq.heappush(events, (core, count, "ready", q))
+                        count += 1
+            elif what == "ready":
+                link = (sends[k]["axis"], sends[k]["s"])
+                heapq.heappush(queue.setdefault(link, []), (rank(k), k))
+                touched.append(link)
+            else:
+                touched.append(k)
+        for link in touched:
+            if queue.get(link) and busy.get(link, 0.0) <= now + 1e-6:
+                _, k = heapq.heappop(queue[link])
+                rate, delay = {"pair": (PAIR_RATE, PAIR_HOP), "core": (1e9, 0.0)}.get(link[0], (RATE, HOP))
+                busy[link] = now + sends[k]["size"] / rate
+                begin[k] = max(ready[k], now - AHEAD)
+                arrive[k] = busy[link] + delay
+                for when, what, item in ((busy[link], "free", link), (arrive[k], "arrive", k)):
+                    heapq.heappush(events, (when, count, what, item))
+                    count += 1
+    return sorted(sends, key=lambda k: (begin[k], k)), arrive
+
+
+def gather_plan(streams=GATHER_STREAMS):
+    sends = gather_sends(streams)
+
+    def rank(k):
+        i, phase, j, s, d = k
+        if phase == 4:
+            return 0.0
+        extra = (0, 6, 0)[i]
+        if phase == 3:
+            return 20 + extra - 0.5 * (SIZE[streams[i][3][2]] // 2 - d)
+        return extra - d
+
+    order, arrive = timeline(sends, rank)
+    return streams, sends, order, arrive
 
 
 def wrap(v, n):
@@ -120,86 +152,98 @@
     pl.semaphore_wait(bar, 7)
 
 
-SENDS, ORDER, ARRIVE, FREE = gather_plan()
-INDEX = {k: n for n, k in enumerate(ORDER)}
-
-
-def gather_kernel(own_ref, items_ref, out_ref, other_items_ref, half, send, recv, local):
+def gather_kernel(plan, own_ref, items_ref, out_ref, other_items_ref, raw, half, send, recv, local):
+    streams, sends, order, arrive = plan
+    index = {k: n for n, k in enumerate(order)}
     me = coords()
     rep = lax.axis_index("rep")
-    half[...] = own_ref[...].reshape(2, 128, 256).astype(jnp.bfloat16)
+    bring = pltpu.make_async_copy(own_ref, raw, local.at[1])
+    bring.start()
+    greet(me, rep)
+    bring.wait()
+    half[...] = raw[...].reshape(2, 128, 256).astype(jnp.bfloat16)
     lines = pl.ds(pl.multiple_of(rep * 64, 64), 64)
-    keep = pltpu.make_async_copy(half.at[:, lines], out_ref.at[me["z"], me["x"], me["y"], :, lines], local)
+    keep = pltpu.make_async_copy(half.at[:, lines], out_ref.at[me["z"], me["x"], me["y"], :, lines], local.at[0])
     keep.start()
-    greet(me, rep)
-
-    def window(key):
-        v = SENDS[key]
-        ksel, row0, rows, order = STREAMS[key[0]]
+    spot = {axis: {off: wrap(me[axis] + off, SIZE[axis]) for off in range(-(SIZE[axis] // 2), SIZE[axis] // 2 + 1)} for axis in AXES}
+    close = {(axis, s): neighbour(me, axis, s) for axis in AXES for s in (1, -1)}
+    pair = (index_of(me), 1 - rep)
+
+    def copy(key):
+        v = sends[key]
+        panels, row0, rows, axes = streams[key[0]]
         where = []
         for axis in AXES:
             off = v["at"][axis]
-            where.append(slice(None) if off is None else wrap(me[axis] + off, SIZE[axis]))
+            if off is not None:
+                where.append(spot[axis][off])
+            elif axis == axes[0] and len(v["h"]) == 1:
+                where.append(pl.ds(SIZE[axis] // 2 * v["h"][0], SIZE[axis] // 2))
+            else:
+                where.append(slice(None))
         row = pl.ds(pl.multiple_of(rep * 64 + row0, 16), rows)
-        cols = slice(None) if len(v["h"]) == 2 else pl.ds(128 * v["h"][0], 128)
-        return tuple(where) + (ksel, row, cols), (ksel, row, cols)
-
-    def copy(key):
-        v = SENDS[key]
-        place, mine = window(key)
-        if key[1] == 4:
-            target = (index_of(me), 1 - rep)
-        else:
-            target = (neighbour(me, v["axis"], v["s"]), rep)
-        src = half.at[mine] if key[1] == 1 and not v["deps"] else out_ref.at[place]
+        place = tuple(where) + (panels, row)
         return pltpu.make_async_remote_copy(
-            src_ref=src, dst_ref=out_ref.at[place], send_sem=send.at[INDEX[key]], recv_sem=recv.at[INDEX[key]],
-            device_id=target, device_id_type=MESH,
+            src_ref=half.at[panels, row] if not v["deps"] else out_ref.at[place],
+            dst_ref=out_ref.at[place],
+            send_sem=send.at[index[key]],
+            recv_sem=recv.at[index[key]],
+            device_id=pair if key[1] == 4 else (close[v["axis"], v["s"]], rep),
+            device_id_type=MESH,
         )
 
     swap = pltpu.make_async_remote_copy(
-        src_ref=items_ref, dst_ref=other_items_ref, send_sem=send.at[len(ORDER)], recv_sem=recv.at[len(ORDER)],
-        device_id=(index_of(me), 1 - rep), device_id_type=MESH,
+        src_ref=items_ref, dst_ref=other_items_ref, send_sem=send.at[len(order)], recv_sem=recv.at[len(order)],
+        device_id=pair, device_id_type=MESH,
     )
-    swap.start()
     done = set()
     kept = False
-    for key in ORDER:
-        for dep in sorted(SENDS[key]["deps"], key=lambda k: ARRIVE[k]):
+    for key in order:
+        for dep in sorted(sends[key]["deps"], key=lambda k: arrive[k]):
             if dep not in done:
                 copy(dep).wait_recv()
                 done.add(dep)
-        if SENDS[key]["deps"] and not kept:
+        if sends[key]["deps"] and not kept:
+            swap.start()
             keep.wait()
             kept = True
         copy(key).start()
-    for key in sorted(ORDER, key=lambda k: ARRIVE[k]):
+    for key in sorted(order, key=lambda k: arrive[k]):
         if key not in done:
             copy(key).wait_recv()
-    for key in ORDER:
+    for key in order:
         copy(key).wait_send()
     swap.wait()
 
 
-def gather_panels(own, items):
-    count = len(ORDER) + 1
+def gather_panels(own, items, plan=gather_plan(), cid=0, name="gather_panels"):
+    count = len(plan[2]) + 1
+    anywhere = pl.BlockSpec(memory_space=pl.ANY)
     return pl.pallas_call(
-        gather_kernel,
+        functools.partial(gather_kernel, plan),
         out_shape=(
             jax.ShapeDtypeStruct((8, 4, 4, 2, 128, 256), jnp.bfloat16),
             jax.ShapeDtypeStruct(items.shape, items.dtype),
         ),
-        in_specs=[pl.BlockSpec(memory_space=pltpu.VMEM), pl.BlockSpec(memory_space=pl.ANY)],
-        out_specs=(pl.BlockSpec(memory_space=pl.ANY), pl.BlockSpec(memory_space=pl.ANY)),
+        in_specs=[anywhere, anywhere],
+        out_specs=(anywhere, anywhere),
         scratch_shapes=[
+            pltpu.VMEM((256, 256), jnp.float32),
             pltpu.VMEM((2, 128, 256), jnp.bfloat16),
             pltpu.SemaphoreType.DMA((count,)),
             pltpu.SemaphoreType.DMA((count,)),
-            pltpu.SemaphoreType.DMA,
+            pltpu.SemaphoreType.DMA((2,)),
         ],
-        name="gather_panels",
-        compiler_params=pltpu.CompilerParams(collective_id=0, has_side_effects=True, vmem_limit_bytes=48 * 2**20),
+        name=name,
+        compiler_params=pltpu.CompilerParams(collective_id=cid, has_side_effects=True, vmem_limit_bytes=56 * 2**20),
     )(own, items)
+
+
+REDUCE_STREAMS = (
+    (slice(0, 2), 48, 16, ("x", "y", "z")),
+    (slice(0, 1), 0, 48, ("y", "z", "x")),
+    (slice(1, 2), 0, 48, ("x", "z", "y")),
+)
 
 
 def reduce_steps(n):
@@ -223,7 +267,7 @@
     for n, off in enumerate(zs):
         tasks[("pair", off)] = dict(kind="pair", deps=[], size=16 * 64 * 256 * 2, rank=n)
     allz = [("pair", off) for off in zs]
-    for i, (ksel, row0, rows, order) in enumerate(STREAMS):
+    for i, (ksel, row0, rows, order) in enumerate(REDUCE_STREAMS):
         a, b, c = order
         na, nb, nc = SIZE[a], SIZE[b], SIZE[c]
         unit = (ksel.stop - ksel.start) * rows * 128 * 2
@@ -251,48 +295,51 @@
             deps = [("sum", i, 2)] + ([("send", i, 3, 0, s, q - 1)] if q else [])
             tasks[("send", i, 3, 0, s, q)] = dict(kind="send", axis=a, s=s, h=h, deps=deps, size=2 * unit * len(h), rank=-9, e=s * e)
         tasks[("sum", i, 3)] = dict(kind="sum", deps=[("sum", i, 2)] + [("send", i, 3, 0, s, na // 2 - 1) for s in (1, -1)], size=unit * 2, rank=-9)
-    done_at, free, order = {}, {}, []
-    left = dict(tasks)
-    for k in [k for k in left if k[0] == "pair"]:
-        v = left.pop(k)
-        begin = free.get("pair", 0.0)
-        free["pair"] = begin + v["size"] / PAIR_RATE
-        done_at[k] = free["pair"] + 0.7
-        order.append(k)
-    now = 0.0
-    while left:
-        best = None
-        for k, v in left.items():
-            if all(d in done_at for d in v["deps"]):
-                ready = max([done_at[d] for d in v["deps"]])
-                link = free.get((v["axis"], v["s"]), 0.0) if v["kind"] == "send" else 0.0
-                begin = max(ready, now)
-                score = (max(begin, link if link > begin + 2.0 else 0.0), v["rank"], -k[-1] if v["kind"] == "send" else -9)
-                if best is None or score < best[0]:
-                    best = (score, k, begin)
-        _, k, begin = best
-        v = left.pop(k)
-        now = begin + 0.05 + v["size"] / 900e3
-        if v["kind"] == "send":
-            link = (v["axis"], v["s"])
-            free[link] = max(now, free.get(link, 0.0)) + v["size"] / RATE
-            done_at[k] = free[link] + HOP
+    for k, v in tasks.items():
+        v["deps"] = list(dict.fromkeys(v["deps"]))
+        if v["kind"] == "pair":
+            v.update(axis="pair", s=0)
         else:
-            done_at[k] = now
-        order.append(k)
-    return tasks, order, done_at, free
-
-
-TASKS, TASK_ORDER, DONE_AT, LINKS = reduce_plan()
+            v["work"] = v["size"] / WORK_RATE
+            if v["kind"] == "sum":
+                v.update(axis="core", s=k)
+    pairs = [k for k in tasks if k[0] == "pair"]
+    order, arrive = timeline(tasks, lambda k: reduce_rank(tasks[k], k))
+    order = pairs + [k for k in order if k[0] != "pair"]
+    placed, final = set(), []
+    def place(k):
+        if k not in placed:
+            for dep in tasks[k]["deps"]:
+                if dep[0] == "sum":
+                    place(dep)
+            placed.add(k)
+            final.append(k)
+    for k in order:
+        place(k)
+    return tasks, final, arrive
+
+
+WORK_RATE = 600e3
+
+
+def reduce_rank(v, k):
+    if v["kind"] == "pair":
+        return v["rank"]
+    if v["kind"] == "sum":
+        return 0.0
+    return (5.0 + 4 * v["rank"], 10.0, 0.0)[k[2] - 1] - k[-1]
+
+
+TASKS, TASK_ORDER, DONE_AT = reduce_plan()
 SEND_INDEX = {k: n for n, k in enumerate([k for k in TASK_ORDER if k[0] != "sum"])}
 
 
 def dims(i):
-    ksel, row0, rows, order = STREAMS[i]
+    ksel, row0, rows, order = REDUCE_STREAMS[i]
     return ksel.stop - ksel.start, rows, tuple(SIZE[x] for x in order)
 
 
-def reduce_kernel(slots_ref, used_ref, user_ref, user_out, grad_out, mine, other, *rest):
+def reduce_kernel(skip_work, skip_pair, slots_ref, used_ref, user_ref, user_out, grad_out, mine, other, *rest):
     bufs = [dict(zip(("s1", "r1", "l1", "s2", "r2", "l2", "s3", "r3"), rest[8 * i: 8 * i + 8])) for i in range(3)]
     total, send, recv, load, last = rest[24:]
     me = coords()
@@ -326,7 +373,7 @@
             device_id=(neighbour(me, v["axis"], s), rep), device_id_type=MESH)
 
     def share(i, offs, n, cols):
-        ksel, row0, rows, order = STREAMS[i]
+        ksel, row0, rows, order = REDUCE_STREAMS[i]
         a, b, c = order
         where = {b: wrap(me[b] + offs[0], SIZE[b]), c: wrap(me[c] + offs[1], SIZE[c]), a: n}
         owner = index_of(where)
@@ -370,7 +417,7 @@
                     return 0
 
                 if phase == 3:
-                    n = wrap(me[STREAMS[i][3][0]] + v["e"], na)
+                    n = wrap(me[REDUCE_STREAMS[i][3][0]] + v["e"], na)
                     for k in range(kk):
                         x = buf["l2"][n, k, :, cols]
                         if got:
@@ -407,7 +454,7 @@
 
             lax.fori_loop(0, na, body, 0)
         else:
-            ksel, row0, rows, order = STREAMS[i]
+            ksel, row0, rows, order = REDUCE_STREAMS[i]
             n = me[order[0]]
             for k in range(kk):
                 x = buf["l2"][n, k]
@@ -421,7 +468,8 @@
     swapped = False
     for key in TASK_ORDER:
         if key[0] == "pair":
-            remote(key).start()
+            if not skip_pair:
+                remote(key).start()
             continue
         if not swapped:
             swap.start()
@@ -431,9 +479,13 @@
                 continue
             if dep[0] == "pair":
                 loads[dep[1]].wait()
+                if skip_pair:
+                    done.add(dep)
+                    continue
             remote(dep).wait_recv()
             done.add(dep)
-        work(key)
+        if not skip_work:
+            work(key)
         if key[0] == "send":
             remote(key).start()
     keep = pltpu.make_async_copy(total, grad_out.at[:, pl.ds(row_mine, 64), :], last.at[2])
@@ -443,6 +495,8 @@
     keep.start()
     give.start()
     for key in SEND_INDEX:
+        if skip_pair and key[0] == "pair":
+            continue
         if key not in done:
             if key[0] == "pair":
                 loads[key[1]].wait()
@@ -453,7 +507,7 @@
     give.wait()
 
 
-def reduce_parts(slots, used, user_part):
+def reduce_parts(slots, used, user_part, skip_work=False, skip_pair=False, cid=1, name='reduce_parts'):
     scratch = [pltpu.VMEM((8, 4, 4, 64, 256), jnp.bfloat16)] * 2
     for i in range(3):
         kk, rows, (na, nb, nc) = dims(i)
@@ -471,7 +525,7 @@
     ]
     anywhere = pl.BlockSpec(memory_space=pl.ANY)
     return pl.pallas_call(
-        reduce_kernel,
+        functools.partial(reduce_kernel, skip_work, skip_pair),
         out_shape=(
             jax.ShapeDtypeStruct(user_part.shape, jnp.float32),
             jax.ShapeDtypeStruct((2, 128, 256), jnp.float32),
@@ -479,15 +533,15 @@
         in_specs=[anywhere, pl.BlockSpec(memory_space=pltpu.SMEM), anywhere],
         out_specs=(anywhere, anywhere),
         scratch_shapes=scratch,
-        name="reduce_parts",
-        compiler_params=pltpu.CompilerParams(collective_id=1, has_side_effects=True, vmem_limit_bytes=56 * 2**20),
+        name=name,
+        compiler_params=pltpu.CompilerParams(collective_id=cid, has_side_effects=True, vmem_limit_bytes=56 * 2**20),
     )(slots.reshape(8, 4, 4, 128, 256), used, user_part)
 
 
-GROUP, RING = 4, 16
-
-
-def tiles_kernel(keys_ref, panels_ref, counts_ref, users_ref, slots_out, user_out, half, vbuf, cbuf, acc, stage, vsem, csem, ssem):
+GROUP, RING = 16, 32
+
+
+def tiles_kernel(keys_ref, panels_ref, counts_ref, users_ref, slots_out, user_out, half, raw, usem, vbuf, cbuf, acc, stage, vsem, csem, ssem):
     tiles = counts_ref.shape[0]
 
     def key(i):
@@ -518,8 +572,11 @@
             c.start()
         return 0
 
+    bring = pltpu.make_async_copy(users_ref, raw, usem)
+    bring.start()
     lax.fori_loop(0, RING, start, 0)
-    half[...] = users_ref[...].astype(jnp.bfloat16)
+    bring.wait()
+    half[...] = raw[...].astype(jnp.bfloat16)
     user_out[...] = jnp.zeros_like(user_out)
     acc[...] = jnp.zeros_like(acc)
 
@@ -592,10 +649,12 @@
             jax.ShapeDtypeStruct((128, 128, 256), jnp.bfloat16),
             jax.ShapeDtypeStruct((8, 128, 256), jnp.float32),
         ),
-        in_specs=[pl.BlockSpec(memory_space=pltpu.SMEM), anywhere, anywhere, whole],
+        in_specs=[pl.BlockSpec(memory_space=pltpu.SMEM), anywhere, anywhere, anywhere],
         out_specs=(anywhere, whole),
         scratch_shapes=[
             pltpu.VMEM((8, 128, 256), jnp.bfloat16),
+            pltpu.VMEM((8, 128, 256), jnp.float32),
+            pltpu.SemaphoreType.DMA,
             pltpu.VMEM((RING, 128, 256), jnp.bfloat16),
             pltpu.VMEM((RING, 128, 128), jnp.bfloat16),
             pltpu.VMEM((128, 256), jnp.float32),
@@ -605,7 +664,7 @@
             pltpu.SemaphoreType.DMA((RING,)),
         ],
         name="tile_parts",
-        compiler_params=pltpu.CompilerParams(vmem_limit_bytes=40 * 2**20),
+        compiler_params=pltpu.CompilerParams(vmem_limit_bytes=58 * 2**20),
         cost_estimate=pl.CostEstimate(flops=128 * 6 * 128 * 128 * 256, bytes_accessed=26 * 2**20, transcendentals=0),
     )(keys, panels, counts, users)
 

time: 162 us -> 141 us (0.87)
  Pallas kernels: 148 us -> 133 us
  local copies, waits for them, and re-layouts: 6 us -> 0.04 us
    pallas_call x1, Pallas kernels: 27.6 us -> 16.6 us  [tile_parts(): pl.pallas_call(tiles_kernel, out_shape=(jax.ShapeDtypeStruct((128, 128, 2...]
    unnamed x20 -> x14, local copies, waits for them, and re-layouts: 6 us -> 0.04 us
    pallas_call x2, Pallas kernels: 121 us -> 117 us  [the longest x1 60.1 us: gather_panels(): pl.pallas_call(functools.partial(gather_kernel, plan), out_shape=(jax.Sha...]
where the time goes in v2:
time: 141 us
  Pallas kernels  133 us (94%)
  other arithmetic  6.77 us (5%)
    pallas_call x1, Pallas kernels, gather_panels(): pl.pallas_call(functools.partial(gather_kernel, plan), out_shape=(jax.Sha...  60.1 us
    pallas_call x1, Pallas kernels, reduce_parts(): pl.pallas_call(functools.partial(reduce_kernel, skip_work, skip_pair), ou...  56.6 us
    pallas_call x1, Pallas kernels, tile_parts(): pl.pallas_call(tiles_kernel, out_shape=(jax.ShapeDtypeStruct((128, 128, 2...  16.6 us
    sub x2, other arithmetic, adagrad(): return (factors - grad / jnp.sqrt(new_accum), new_accum)  4.58 us

profile of v2, /device:TPU:1, one launch (start us, length us, event | category | flops | bytes accessed | tf_op | source)
XLA Modules:
  0.0 140.9 jit_solution(8380826773535030820)
XLA Ops:
  0.6 0.7 bitcast_add_fusion
  1.3 0.2 convert_reduce_fusion
  1.5 0.6 select_reduce_fusion.keys_ref
  2.1 60.1 %gather_panels.1 = (bf16[8,4,4,2,128,256]{5,4,3,2,1,0:T(8,128)(2,1)}, s32[1,128]{1,0:T(1,128)}) custom-call(f32[256,256]{1,0:T(8,128)} %own_ref.1, s32[1,128]{1,0:T(1,128)} %bitcast.33), custom_call_target="tpu_custom_call" | custom-call | tf_op jit(solution)/shard_map/gather_panels/pallas_call | solution.py:222
  62.2 0.0 copy-start.5
  62.3 0.0 copy-start.6
  62.3 16.6 %tile_parts.1 = (bf16[128,128,256]{2,1,0:T(8,128)(2,1)}, f32[8,128,256]{2,1,0:T(8,128)}) custom-call(s32[128]{0:T(128)} %select_reduce_fusion.keys_ref, bf16[256,128,256]{2,1,0:T(8,128)(2,1)} %bitcast.28, bf16[128,128,128]{2,1,0:T(8,128)(2,1)} %bitcast.32, f32[8,128,256]{2,1,0:T(8,128)} %bitcast.30), custom_call_target="tpu_custom_call" | custom-call | flops 3221225472 | bytes 27262976 | tf_op jit(solution)/shard_map/tile_parts/pallas_call | solution.py:646
  78.9 0.0 copy-start
  78.9 0.0 copy-start.1
  78.9 0.0 copy-start.3
  78.9 0.0 copy-start.2
  79.0 0.0 copy-start.4
  79.0 0.0 copy-done.5
  79.0 0.0 copy-done.6
  79.0 0.1 fusion.2
  79.1 0.6 convert_element_type.7.used_ref
  79.7 56.6 %reduce_parts.1 = (f32[1024,256]{1,0:T(8,128)}, f32[2,128,256]{2,1,0:T(8,128)}) custom-call(bf16[8,4,4,128,256]{4,3,2,1,0:T(8,128)(2,1)} %bitcast.29, s32[2,256]{1,0:T(2,128)} %convert_element_type.7.used_ref, f32[1024,256]{1,0:T(8,128)} %bitcast.31), custom_call_target="tpu_custom_call" | custom-call | tf_op jit(solution)/shard_map/reduce_parts/pallas_call | solution.py:527
  136.3 0.0 copy-done
  136.3 0.0 copy-done.1
  136.3 0.0 copy-done.3
  136.3 2.8 %multiply_subtract_fusion = (f32[1024,256]{1,0:T(8,128)}, f32[1024,256]{1,0:T(8,128)}) fusion(f32[1024,256]{1,0:T(8,128)S(1)} %copy-done, f32[1024,256]{1,0:T(8,128)} %get-tuple-element.14, f32[8,128,256]{2,1,0:T(8,128)S(1)} %copy-done.1, f32[1024,256]{1,0:T(8,128)S(1)} %copy-done.3), kind=kLoop, calls=%fused_computation | loop fusion | flops 1310720 | bytes 6291456 | tf_op jit(solution)/shard_map/sub | solution.py:681
  139.1 0.0 copy-done.2
  139.1 0.0 copy-done.4
  139.1 1.8 %fusion.1 = (f32[256,256]{1,0:T(8,128)}, f32[256,256]{1,0:T(8,128)}) fusion(f32[256,256]{1,0:T(8,128)S(1)} %copy-done.2, f32[2,128,256]{2,1,0:T(8,128)} %get-tuple-element.15, f32[256,256]{1,0:T(8,128)S(1)} %copy-done.4), kind=kLoop, calls=%fused_computation.5 | loop fusion | flops 262144 | bytes 1310720 | tf_op jit(solution)/shard_map/sub | solution.py:681
  (1 shorter events, 0.0 us)
Async XLA Ops:
  62.2 16.7 %copy-start.5 = (s32[1,1,128]{2,1,0:T(1,128)S(1)}, s32[1,1,128]{2,1,0:T(1,128)}, u32[]{:S(2)}) copy-start(s32[1,1,128]{2,1,0:T(1,128)} %param.14) | copy-start | bytes 1540
  62.3 16.7 %copy-start.6 = (s32[1,128]{1,0:T(1,128)S(1)}, s32[1,128]{1,0:T(1,128)}, u32[]{:S(2)}) copy-start(s32[1,128]{1,0:T(1,128)} %get-tuple-element.13) | copy-start | bytes 1540
  78.9 57.4 %copy-start = (f32[1024,256]{1,0:T(8,128)S(1)}, f32[1024,256]{1,0:T(8,128)}, u32[]{:S(2)}) copy-start(f32[1024,256]{1,0:T(8,128)} %param.8) | copy-start | bytes 3145732
  78.9 57.4 %copy-start.1 = (f32[8,128,256]{2,1,0:T(8,128)S(1)}, f32[8,128,256]{2,1,0:T(8,128)}, u32[]{:S(2)}) copy-start(f32[8,128,256]{2,1,0:T(8,128)} %get-tuple-element.11) | copy-start | bytes 3145732
  78.9 57.4 %copy-start.3 = (f32[1024,256]{1,0:T(8,128)S(1)}, f32[1024,256]{1,0:T(8,128)}, u32[]{:S(2)}) copy-start(f32[1024,256]{1,0:T(8,128)} %param.9) | copy-start | bytes 3145732
  78.9 60.2 %copy-start.2 = (f32[256,256]{1,0:T(8,128)S(1)}, f32[256,256]{1,0:T(8,128)}, u32[]{:S(2)}) copy-start(f32[256,256]{1,0:T(8,128)} %own_ref.1) | copy-start | bytes 786436
  79.0 60.2 %copy-start.4 = (f32[256,256]{1,0:T(8,128)S(1)}, f32[256,256]{1,0:T(8,128)}, u32[]{:S(2)}) copy-start(f32[256,256]{1,0:T(8,128)} %param.11) | copy-start | bytes 786436

commit v3 on v2

--- a/solution.py
+++ b/solution.py
@@ -12,11 +12,18 @@
 AXES = ("z", "x", "y")
 SIZE = {"z": 8, "x": 4, "y": 4}
 GATHER_STREAMS = (
-    (slice(0, 2), 48, 16, ("x", "y", "z")),
-    (slice(0, 1), 0, 48, ("y", "z", "x")),
-    (slice(1, 2), 0, 48, ("x", "z", "y")),
+    (
+        (slice(0, 2), 48, 16, ("x", "y", "z")),
+        (slice(0, 1), 0, 48, ("y", "z", "x")),
+        (slice(1, 2), 0, 48, ("x", "z", "y")),
+    ),
+    (
+        (slice(1, 2), 48, 16, ("x", "y", "z")),
+        (slice(0, 1), 0, 64, ("y", "z", "x")),
+        (slice(1, 2), 0, 48, ("x", "z", "y")),
+    ),
 )
-RATE, PAIR_RATE, HOP, PAIR_HOP, ISSUE, AHEAD = 45e3, 500e3, 1.7, 0.8, 0.07, 2.5
+RATE, PAIR_RATE, HOP, PAIR_HOP, ISSUE, AHEAD = 43e3, 500e3, 1.7, 0.8, 0.07, 2.5
 
 
 def signed(j, n):
@@ -38,14 +45,15 @@
         a, b, c = order
         unit = (panels.stop - panels.start) * rows * 128 * 2
         na, nb, nc = SIZE[a], SIZE[b], SIZE[c]
-        first = [(s, d, (0, 1)) for s, d, h in ring_steps(na) if s == 1 or d < na // 2 - 1]
-        near = [(i, 1, 0, s, d) for s, d, h in first]
+        first = [(s, d) for d in range(na // 2) for s in (1, -1) if (s == 1) == (i % 2 == 0) or d < na // 2 - 1]
+        near = [(i, 1, 0, s, d) for s, d in first]
 
         def add(key, axis, h, deps, size, at):
             sends[key] = dict(axis=axis, s=key[3], h=h, deps=deps, size=size, at=at)
 
-        for s, d, h in first:
-            add((i, 1, 0, s, d), a, h, [] if d == 0 else [(i, 1, 0, s, d - 1)], unit * 2, {a: -s * d, b: 0, c: 0})
+        for s, d in first:
+            add((i, 1, 0, s, d), a, (0, 1), [], unit * 2, {a: 0, b: 0, c: 0})
+            sends[i, 1, 0, s, d].update(hops=d + 1)
         for s, d, h in ring_steps(nb):
             deps = near if d == 0 else [(i, 2, 0, s, d - 1)]
             add((i, 2, 0, s, d), b, h, deps, unit * len(h) * na, {a: None, b: -s * d, c: 0})
@@ -99,25 +107,27 @@
             if queue.get(link) and busy.get(link, 0.0) <= now + 1e-6:
                 _, k = heapq.heappop(queue[link])
                 rate, delay = {"pair": (PAIR_RATE, PAIR_HOP), "core": (1e9, 0.0)}.get(link[0], (RATE, HOP))
-                busy[link] = now + sends[k]["size"] / rate
+                hops = sends[k].get("hops", 1)
+                busy[link] = now + sends[k]["size"] * hops / rate
                 begin[k] = max(ready[k], now - AHEAD)
-                arrive[k] = busy[link] + delay
+                arrive[k] = busy[link] + delay + 0.4 * (hops - 1)
                 for when, what, item in ((busy[link], "free", link), (arrive[k], "arrive", k)):
                     heapq.heappush(events, (when, count, what, item))
                     count += 1
     return sorted(sends, key=lambda k: (begin[k], k)), arrive
 
 
-def gather_plan(streams=GATHER_STREAMS):
+def gather_plan(streams):
     sends = gather_sends(streams)
 
     def rank(k):
         i, phase, j, s, d = k
         if phase == 4:
             return 0.0
-        extra = (0, 6, 0)[i]
+        extra = (0, 0, 2)[i]
         if phase == 3:
-            return 20 + extra - 0.5 * (SIZE[streams[i][3][2]] // 2 - d)
+            b, c = streams[i][3][1:]
+            return 20 + extra - 2 * (SIZE[c] // 2 - d) + 0.3 * min(j, SIZE[b] - j)
         return extra - d
 
     order, arrive = timeline(sends, rank)
@@ -143,23 +153,43 @@
     return index_of(c)
 
 
-def greet(me, rep):
+def greet(me, rep, far):
     bar = pltpu.get_barrier_semaphore()
-    for axis in AXES:
-        for s in (1, -1):
-            pl.semaphore_signal(bar, inc=1, device_id=(neighbour(me, axis, s), rep), device_id_type=MESH)
+    peers = [(axis, s) for axis in AXES for s in (1, -1)]
+    peers += [(axis, s) for axis in far for s in range(2, SIZE[axis] - 1)]
+    for axis, s in peers:
+        pl.semaphore_signal(bar, inc=1, device_id=(neighbour(me, axis, s), rep), device_id_type=MESH)
     pl.semaphore_signal(bar, inc=1, device_id=(index_of(me), 1 - rep), device_id_type=MESH)
-    pl.semaphore_wait(bar, 7)
-
-
-def gather_kernel(plan, own_ref, items_ref, out_ref, other_items_ref, raw, half, send, recv, local):
-    streams, sends, order, arrive = plan
-    index = {k: n for n, k in enumerate(order)}
+    pl.semaphore_wait(bar, len(peers) + 1)
+
+
+def sort_keys(items, blocks):
+    n = items.shape[-1]
+    square = (n, n)
+    key = (items * n + lax.broadcasted_iota(jnp.int32, (1, n), 1)) * 8 + blocks
+    across = jnp.broadcast_to(key, square)
+    down = jnp.transpose(across)
+    rank = jnp.sum((down < across).astype(jnp.int32), axis=0, keepdims=True)
+    rank_down = jnp.transpose(jnp.broadcast_to(rank, square))
+    place = lax.broadcasted_iota(jnp.int32, square, 1)
+    return jnp.sum(jnp.where(rank_down == place, down, 0), axis=0, keepdims=True)
+
+
+def used_panels(items, count):
+    down = jnp.transpose(jnp.broadcast_to(items, (items.shape[-1],) * 2))
+    out = []
+    for start in range(0, count, 128):
+        panel = lax.broadcasted_iota(jnp.int32, down.shape, 1) + start
+        out.append(jnp.max((down == panel).astype(jnp.int32), axis=0, keepdims=True))
+    return jnp.concatenate(out, axis=1)
+
+
+def gather_kernel(plans, own_ref, items_ref, blocks_ref, out_ref, keys_ref, used_ref, raw, half, other_items, send, recv, pair_recv, swap_sem, local):
     me = coords()
     rep = lax.axis_index("rep")
     bring = pltpu.make_async_copy(own_ref, raw, local.at[1])
     bring.start()
-    greet(me, rep)
+    greet(me, rep, sorted({stream[3][0] for streams, _, _, _ in plans for stream in streams}))
     bring.wait()
     half[...] = raw[...].reshape(2, 128, 256).astype(jnp.bfloat16)
     lines = pl.ds(pl.multiple_of(rep * 64, 64), 64)
@@ -168,8 +198,13 @@
     spot = {axis: {off: wrap(me[axis] + off, SIZE[axis]) for off in range(-(SIZE[axis] // 2), SIZE[axis] // 2 + 1)} for axis in AXES}
     close = {(axis, s): neighbour(me, axis, s) for axis in AXES for s in (1, -1)}
     pair = (index_of(me), 1 - rep)
-
-    def copy(key):
+    swap = pltpu.make_async_remote_copy(
+        src_ref=items_ref, dst_ref=other_items, send_sem=swap_sem.at[0], recv_sem=swap_sem.at[1],
+        device_id=pair, device_id_type=MESH,
+    )
+
+    def copy(side, key):
+        streams, sends, order, arrive = plans[side]
         v = sends[key]
         panels, row0, rows, axes = streams[key[0]]
         where = []
@@ -181,66 +216,90 @@
                 where.append(pl.ds(SIZE[axis] // 2 * v["h"][0], SIZE[axis] // 2))
             else:
                 where.append(slice(None))
-        row = pl.ds(pl.multiple_of(rep * 64 + row0, 16), rows)
+        row = pl.ds(side * 64 + row0, rows)
         place = tuple(where) + (panels, row)
+        number = order.index(key)
+        arrival = recv.at[number]
+        if key[1] == 4:
+            target = pair
+            arrival = pair_recv.at[side, number]
+        elif key[1] == 1:
+            target = (neighbour(me, v["axis"], v["s"] * (key[4] + 1)), rep)
+        else:
+            target = (close[v["axis"], v["s"]], rep)
         return pltpu.make_async_remote_copy(
             src_ref=half.at[panels, row] if not v["deps"] else out_ref.at[place],
             dst_ref=out_ref.at[place],
-            send_sem=send.at[index[key]],
-            recv_sem=recv.at[index[key]],
-            device_id=pair if key[1] == 4 else (close[v["axis"], v["s"]], rep),
+            send_sem=send.at[number],
+            recv_sem=arrival,
+            device_id=target,
             device_id_type=MESH,
         )
 
-    swap = pltpu.make_async_remote_copy(
-        src_ref=items_ref, dst_ref=other_items_ref, send_sem=send.at[len(order)], recv_sem=recv.at[len(order)],
-        device_id=pair, device_id_type=MESH,
-    )
-    done = set()
-    kept = False
-    for key in order:
-        for dep in sorted(sends[key]["deps"], key=lambda k: arrive[k]):
-            if dep not in done:
-                copy(dep).wait_recv()
-                done.add(dep)
-        if sends[key]["deps"] and not kept:
-            swap.start()
-            keep.wait()
-            kept = True
-        copy(key).start()
-    for key in sorted(order, key=lambda k: arrive[k]):
-        if key not in done:
-            copy(key).wait_recv()
-    for key in order:
-        copy(key).wait_send()
-    swap.wait()
-
-
-def gather_panels(own, items, plan=gather_plan(), cid=0, name="gather_panels"):
-    count = len(plan[2]) + 1
+    def run(side):
+        streams, sends, order, arrive = plans[side]
+        done = set()
+        kept = False
+        for key in order:
+            for dep in sorted(sends[key]["deps"], key=lambda k: arrive[k]):
+                if dep not in done:
+                    copy(side, dep).wait_recv()
+                    done.add(dep)
+            if sends[key]["deps"] and not kept:
+                keep.wait()
+                kept = True
+            copy(side, key).start()
+            if key[1] == 3 and "swap" not in done:
+                done.add("swap")
+                swap.start()
+                keys_ref[...] = sort_keys(items_ref[...], blocks_ref[...])
+                used_ref[0:1, :] = used_panels(items_ref[...], used_ref.shape[1])
+        for key in sorted(order, key=lambda k: arrive[k]):
+            if key[1] != 4 and key not in done:
+                copy(side, key).wait_recv()
+        swap.wait()
+        used_ref[1:2, :] = used_panels(other_items[...], used_ref.shape[1])
+        for key in plans[1 - side][2]:
+            if key[1] == 4:
+                copy(1 - side, key).wait_recv()
+        for key in order:
+            copy(side, key).wait_send()
+
+    for side in range(2):
+        pl.when(rep == side)(functools.partial(run, side))
+
+
+def gather_panels(own, items, blocks, cid=0, name="gather_panels"):
+    plans = tuple(gather_plan(streams) for streams in GATHER_STREAMS)
+    count = max(len(plan[2]) for plan in plans)
     anywhere = pl.BlockSpec(memory_space=pl.ANY)
+    whole = pl.BlockSpec(memory_space=pltpu.VMEM)
     return pl.pallas_call(
-        functools.partial(gather_kernel, plan),
+        functools.partial(gather_kernel, plans),
         out_shape=(
             jax.ShapeDtypeStruct((8, 4, 4, 2, 128, 256), jnp.bfloat16),
-            jax.ShapeDtypeStruct(items.shape, items.dtype),
+            jax.ShapeDtypeStruct(items.shape, jnp.int32),
+            jax.ShapeDtypeStruct((2, 256), jnp.int32),
         ),
-        in_specs=[anywhere, anywhere],
-        out_specs=(anywhere, anywhere),
+        in_specs=[anywhere, whole, whole],
+        out_specs=(anywhere, whole, whole),
         scratch_shapes=[
             pltpu.VMEM((256, 256), jnp.float32),
             pltpu.VMEM((2, 128, 256), jnp.bfloat16),
+            pltpu.VMEM(items.shape, jnp.int32),
             pltpu.SemaphoreType.DMA((count,)),
             pltpu.SemaphoreType.DMA((count,)),
+            pltpu.SemaphoreType.DMA((2, count)),
+            pltpu.SemaphoreType.DMA((2,)),
             pltpu.SemaphoreType.DMA((2,)),
         ],
         name=name,
         compiler_params=pltpu.CompilerParams(collective_id=cid, has_side_effects=True, vmem_limit_bytes=56 * 2**20),
-    )(own, items)
+    )(own, items, blocks)
 
 
 REDUCE_STREAMS = (
-    (slice(0, 2), 48, 16, ("x", "y", "z")),
+    (slice(0, 2), 48, 16, ("y", "x", "z")),
     (slice(0, 1), 0, 48, ("y", "z", "x")),
     (slice(1, 2), 0, 48, ("x", "z", "y")),
 )
@@ -252,6 +311,10 @@
         for s in (1, -1):
             out.append((s, q, n // 2 - q, ((0,) if s == 1 else (1,)) if q == 0 else (0, 1)))
     return out
+
+
+def direct(i, n):
+    return [(s, q, s * (q + 1)) for q in range(n // 2) for s in (1, -1) if (s == 1) == (i % 2 == 0) or q < n // 2 - 1]
 
 
 def far_first(n):
@@ -291,10 +354,9 @@
             deps = [("sum", i, 1, line)] + ([("send", i, 2, 0, s, q - 1)] if q else [])
             tasks[("send", i, 2, 0, s, q)] = dict(kind="send", axis=b, s=s, h=h, deps=deps, size=unit * len(h) * na, rank=-5, e=line)
         tasks[("sum", i, 2)] = dict(kind="sum", deps=[("sum", i, 1, 0)] + [("send", i, 2, 0, s, nb // 2 - 1) for s in (1, -1)], size=unit * 2 * na, rank=-5)
-        for s, q, e, h in reduce_steps(na):
-            deps = [("sum", i, 2)] + ([("send", i, 3, 0, s, q - 1)] if q else [])
-            tasks[("send", i, 3, 0, s, q)] = dict(kind="send", axis=a, s=s, h=h, deps=deps, size=2 * unit * len(h), rank=-9, e=s * e)
-        tasks[("sum", i, 3)] = dict(kind="sum", deps=[("sum", i, 2)] + [("send", i, 3, 0, s, na // 2 - 1) for s in (1, -1)], size=unit * 2, rank=-9)
+        for s, q, e in direct(i, na):
+            tasks[("send", i, 3, 0, s, q)] = dict(kind="send", axis=a, s=s, h=(0, 1), deps=[("sum", i, 2)], size=4 * unit, rank=-9, e=e, hops=q + 1)
+        tasks[("sum", i, 3)] = dict(kind="sum", deps=[("sum", i, 2)] + [("send", i, 3, 0, s, q) for s, q, e in direct(i, na)], size=unit * 2, rank=-9)
     for k, v in tasks.items():
         v["deps"] = list(dict.fromkeys(v["deps"]))
         if v["kind"] == "pair":
@@ -327,7 +389,7 @@
         return v["rank"]
     if v["kind"] == "sum":
         return 0.0
-    return (5.0 + 4 * v["rank"], 10.0, 0.0)[k[2] - 1] - k[-1]
+    return (10.0 + v["rank"], 0.0, 0.0)[k[2] - 1] + (0.0, 12.0, 12.0)[k[1]]
 
 
 TASKS, TASK_ORDER, DONE_AT = reduce_plan()
@@ -339,7 +401,7 @@
     return ksel.stop - ksel.start, rows, tuple(SIZE[x] for x in order)
 
 
-def reduce_kernel(skip_work, skip_pair, slots_ref, used_ref, user_ref, user_out, grad_out, mine, other, *rest):
+def reduce_kernel(slots_ref, used_ref, user_ref, user_out, grad_out, mine, other, *rest):
     bufs = [dict(zip(("s1", "r1", "l1", "s2", "r2", "l2", "s3", "r3"), rest[8 * i: 8 * i + 8])) for i in range(3)]
     total, send, recv, load, last = rest[24:]
     me = coords()
@@ -351,7 +413,7 @@
     for n, off in enumerate(far_first(8)):
         loads[off] = pltpu.make_async_copy(slots_ref.at[zof[off], :, :, pl.ds(row_mine, 64), :], mine.at[zof[off]], load.at[n])
         loads[off].start()
-    greet(me, rep)
+    greet(me, rep, sorted({stream[3][0] for stream in REDUCE_STREAMS}))
     pair = (index_of(me), 1 - rep)
 
     def remote(key):
@@ -370,7 +432,7 @@
         return pltpu.make_async_remote_copy(
             src_ref=bufs[i]["s%d" % phase].at[at + tail], dst_ref=bufs[i]["r%d" % phase].at[at + tail],
             send_sem=send.at[SEND_INDEX[key]], recv_sem=recv.at[SEND_INDEX[key]],
-            device_id=(neighbour(me, v["axis"], s), rep), device_id_type=MESH)
+            device_id=(neighbour(me, v["axis"], v["e"] if phase == 3 else s), rep), device_id_type=MESH)
 
     def share(i, offs, n, cols):
         ksel, row0, rows, order = REDUCE_STREAMS[i]
@@ -395,6 +457,10 @@
         if key[0] == "send":
             _, i, phase, j, s, q = key
             side = 0 if s == 1 else 1
+            if phase == 3:
+                n = wrap(me[REDUCE_STREAMS[i][3][0]] + v["e"], na)
+                buf["s3"][side, q] = buf["l2"][n]
+                return
             for h in ((0, 1) if (q == 1) else (None,)):
                 cols = pl.ds(128 * h, 128) if h is not None else (pl.ds(0, 256) if len(v["h"]) == 2 else pl.ds(128 * v["h"][0], 128))
                 got = q >= 2 or (q == 1 and h == side)
@@ -416,15 +482,7 @@
                             buf["s2"][side, q, n, k, :, cols] = x.astype(jnp.bfloat16)
                     return 0
 
-                if phase == 3:
-                    n = wrap(me[REDUCE_STREAMS[i][3][0]] + v["e"], na)
-                    for k in range(kk):
-                        x = buf["l2"][n, k, :, cols]
-                        if got:
-                            x = x + buf["r3"][side, q - 1, k, :, cols]
-                        buf["s3"][side, q, k, :, cols] = x
-                else:
-                    lax.fori_loop(0, na, body, 0)
+                lax.fori_loop(0, na, body, 0)
             return
         phase = key[2]
         end = {1: nc, 2: nb, 3: na}[phase] // 2 - 1
@@ -458,8 +516,8 @@
             n = me[order[0]]
             for k in range(kk):
                 x = buf["l2"][n, k]
-                for side in range(2):
-                    x = x + buf["r3"][side, end, k]
+                for s, q, e in direct(i, na):
+                    x = x + buf["r3"][0 if s == 1 else 1, q, k]
                 total[ksel.start + k, pl.ds(row0, rows), :] = x
 
     swap = pltpu.make_async_remote_copy(
@@ -468,8 +526,7 @@
     swapped = False
     for key in TASK_ORDER:
         if key[0] == "pair":
-            if not skip_pair:
-                remote(key).start()
+            remote(key).start()
             continue
         if not swapped:
             swap.start()
@@ -479,13 +536,9 @@
                 continue
             if dep[0] == "pair":
                 loads[dep[1]].wait()
-                if skip_pair:
-                    done.add(dep)
-                    continue
             remote(dep).wait_recv()
             done.add(dep)
-        if not skip_work:
-            work(key)
+        work(key)
         if key[0] == "send":
             remote(key).start()
     keep = pltpu.make_async_copy(total, grad_out.at[:, pl.ds(row_mine, 64), :], last.at[2])
@@ -495,8 +548,6 @@
     keep.start()
     give.start()
     for key in SEND_INDEX:
-        if skip_pair and key[0] == "pair":
-            continue
         if key not in done:
             if key[0] == "pair":
                 loads[key[1]].wait()
@@ -507,7 +558,7 @@
     give.wait()
 
 
-def reduce_parts(slots, used, user_part, skip_work=False, skip_pair=False, cid=1, name='reduce_parts'):
+def reduce_parts(slots, used, user_part, cid=1, name='reduce_parts'):
     scratch = [pltpu.VMEM((8, 4, 4, 64, 256), jnp.bfloat16)] * 2
     for i in range(3):
         kk, rows, (na, nb, nc) = dims(i)
@@ -525,7 +576,7 @@
     ]
     anywhere = pl.BlockSpec(memory_space=pl.ANY)
     return pl.pallas_call(
-        functools.partial(reduce_kernel, skip_work, skip_pair),
+        reduce_kernel,
         out_shape=(
             jax.ShapeDtypeStruct(user_part.shape, jnp.float32),
             jax.ShapeDtypeStruct((2, 128, 256), jnp.float32),
@@ -669,31 +720,42 @@
     )(keys, panels, counts, users)
 
 
-def sorted_keys(items, blocks):
-    key = (items * 128 + jnp.arange(items.shape[0], dtype=jnp.int32)) * 8 + blocks
-    rank = jnp.sum((key[None, :] < key[:, None]).astype(jnp.int32), axis=1)
-    place = jnp.arange(items.shape[0], dtype=jnp.int32)
-    return jnp.sum(jnp.where(rank[None, :] == place[:, None], key[None, :], 0), axis=1)
-
-
-def adagrad(factors, accum, grad):
-    new_accum = accum + grad * grad
-    return factors - grad / jnp.sqrt(new_accum), new_accum
+def adagrad_kernel(part, other, users, user_accum, grad, items, item_accum, new_users, new_user_accum, new_items, new_item_accum):
+    for g, factors, accum, new, new_accum in (
+        (part[...] + other[...], users, user_accum, new_users, new_user_accum),
+        (grad[...], items, item_accum, new_items, new_item_accum),
+    ):
+        total = accum[...] + g * g
+        new_accum[...] = total
+        new[...] = factors[...] - g / jnp.sqrt(total)
+
+
+def adagrad(part, other, users, user_accum, grad, items, item_accum, steps=4):
+    def rows(x):
+        return pl.BlockSpec((x.shape[0] // steps, x.shape[1]), lambda n: (n, 0))
+
+    args = (part, other, users, user_accum, grad, items, item_accum)
+    outs = (users, user_accum, items, item_accum)
+    return pl.pallas_call(
+        adagrad_kernel,
+        grid=(steps,),
+        out_shape=tuple(jax.ShapeDtypeStruct(x.shape, x.dtype) for x in outs),
+        in_specs=[rows(x) for x in args],
+        out_specs=tuple(rows(x) for x in outs),
+        name="adagrad",
+        compiler_params=pltpu.CompilerParams(vmem_limit_bytes=56 * 2**20),
+    )(*args)
 
 
 def local(user_factors, user_accum, item_factors, item_accum, tile_counts, tile_user, tile_item, send_list):
     counts = tile_counts[0, 0]
-    items = tile_item[0, 0]
-    keys = sorted_keys(items, tile_user[0, 0])
-    panels, other_items = gather_panels(item_factors, items[None, :])
-    both = jnp.stack([items, other_items[0]])
-    used = jnp.any(both[:, :, None] == jnp.arange(256, dtype=jnp.int32), axis=1).astype(jnp.int32)
-    slots, user_part = tile_parts(keys, panels.reshape(256, 128, 256), counts, user_factors.reshape(8, 128, 256))
+    panels, keys, used = gather_panels(item_factors, tile_item[0], tile_user[0])
+    slots, user_part = tile_parts(keys[0], panels.reshape(256, 128, 256), counts, user_factors.reshape(8, 128, 256))
     other_user, item_grad = reduce_parts(slots, used, user_part.reshape(1024, 256))
-    user_grad = user_part.reshape(1024, 256) + other_user
-    new_users, new_user_accum = adagrad(user_factors, user_accum, user_grad)
-    new_items, new_item_accum = adagrad(item_factors, item_accum, item_grad.reshape(256, 256))
-    return new_users, new_user_accum, new_items, new_item_accum
+    return adagrad(
+        user_part.reshape(1024, 256), other_user, user_factors, user_accum,
+        item_grad.reshape(256, 256), item_factors, item_accum,
+    )
 
 
 def solution(mesh):

time: 141 us -> 137 us (0.972)
  other arithmetic: 6.77 us -> 0 us
  Pallas kernels: 133 us -> 135 us
    sub x2 -> x0, other arithmetic: 4.58 us -> none  [adagrad(): return (factors - grad / jnp.sqrt(new_accum), new_accum)]
    pallas_call x2 -> x3, Pallas kernels: 117 us -> 118 us  [the longest x1 61 us: gather_panels(): pl.pallas_call(functools.partial(gather_kernel, plans), out_shape=(jax.Sh...]
where the time goes in v3:
time: 137 us; the launch traced here: 136 us
  Pallas kernels  135 us (99%)
    pallas_call x1, Pallas kernels, gather_panels(): pl.pallas_call(functools.partial(gather_kernel, plans), out_shape=(jax.Sh...  61 us
    pallas_call x1, Pallas kernels, reduce_parts(): pl.pallas_call(reduce_kernel, out_shape=(jax.ShapeDtypeStruct(user_part.s...  52.8 us
    pallas_call x1, Pallas kernels, tile_parts(): pl.pallas_call(tiles_kernel, out_shape=(jax.ShapeDtypeStruct((128, 128, 2...  16.9 us
    pallas_call x1, Pallas kernels, adagrad(): pl.pallas_call(adagrad_kernel, grid=(steps,), out_shape=tuple((jax.ShapeD...  4.29 us

profile of v3, /device:TPU:1, one launch (start us, length us, event | category | flops | bytes accessed | tf_op | source)
XLA Modules:
  0.0 135.8 jit_solution(17708835226642960646)
XLA Ops:
  0.6 61.0 %gather_panels.1 = (bf16[8,4,4,2,128,256]{5,4,3,2,1,0:T(8,128)(2,1)}, s32[1,128]{1,0:T(1,128)}, s32[2,256]{1,0:T(2,128)}) custom-call(f32[256,256]{1,0:T(8,128)} %items.1, s32[1,128]{1,0:T(1,128)} %bitcast.17, s32[1,128]{1,0:T(1,128)} %bitcast.18), custom_call_target="tpu_custom_call" | custom-call | tf_op jit(solution)/shard_map/gather_panels/pallas_call | solution.py:277
  61.6 16.9 %tile_parts.1 = (bf16[128,128,256]{2,1,0:T(8,128)(2,1)}, f32[8,128,256]{2,1,0:T(8,128)}) custom-call(s32[128]{0:T(128)} %bitcast.16, bf16[256,128,256]{2,1,0:T(8,128)(2,1)} %bitcast.9, bf16[128,128,128]{2,1,0:T(8,128)(2,1)} %bitcast.14, f32[8,128,256]{2,1,0:T(8,128)} %bitcast.11), custom_call_target="tpu_custom_call" | custom-call | flops 3221225472 | bytes 27262976 | tf_op jit(solution)/shard_map/tile_parts/pallas_call | solution.py:697
  78.5 52.8 %reduce_parts.1 = (f32[1024,256]{1,0:T(8,128)}, f32[2,128,256]{2,1,0:T(8,128)}) custom-call(bf16[8,4,4,128,256]{4,3,2,1,0:T(8,128)(2,1)} %bitcast.10, s32[2,256]{1,0:T(2,128)} %get-tuple-element.15.used_ref, f32[1024,256]{1,0:T(8,128)} %bitcast.12), custom_call_target="tpu_custom_call" | custom-call | tf_op jit(solution)/shard_map/reduce_parts/pallas_call | solution.py:578
  131.3 4.3 %adagrad.1 = (f32[1024,256]{1,0:T(8,128)}, f32[1024,256]{1,0:T(8,128)}, f32[256,256]{1,0:T(8,128)}, f32[256,256]{1,0:T(8,128)}) custom-call(f32[1024,256]{1,0:T(8,128)} %bitcast.13, f32[1024,256]{1,0:T(8,128)} %get-tuple-element.16.other, f32[1024,256]{1,0:T(8,128)} %users.1, f32[1024,256]{1,0:T(8,128)} %user_accum.1, f32[256,256]{1,0:T(8,128)} %bitcast.15, ...), custom_call_target="tpu_custom_call" | custom-call | tf_op jit(solution)/shard_map/adagrad/pallas_call | solution.py:739

commit v4 on v3

--- a/solution.py
+++ b/solution.py
@@ -23,6 +23,7 @@
         (slice(1, 2), 0, 48, ("x", "z", "y")),
     ),
 )
+PAIR_LOAD = 5 / 3
 RATE, PAIR_RATE, HOP, PAIR_HOP, ISSUE, AHEAD = 43e3, 500e3, 1.7, 0.8, 0.07, 2.5
 
 
@@ -68,8 +69,19 @@
             for s, d, h in ring_steps(nc):
                 deps = line if d == 0 else [(i, 3, j, s, d - 1)]
                 add((i, 3, j, s, d), c, h, deps, unit * len(h) * na, {a: None, b: off, c: -s * d})
-            deps = line + [(i, 3, j, s, d) for s, d, h in ring_steps(nc)]
-            add((i, 4, j, 0, 0), "pair", (0, 1), deps, unit * 2 * na * nc, {a: None, b: off, c: None})
+            if abs(off) < nb // 2:
+                deps = line + [(i, 3, j, s, d) for s, d, h in ring_steps(nc)]
+                add((i, 4, j, 0, 0), "pair", (0, 1), deps, unit * 2 * na * nc * PAIR_LOAD, {a: None, b: off, c: None})
+                continue
+            for m in range(nc):
+                far = signed(m, nc)
+                if far == 0:
+                    deps = line
+                elif far == nc // 2:
+                    deps = [(i, 3, j, s, nc // 2 - 1) for s in (1, -1)]
+                else:
+                    deps = [(i, 3, j, -1 if far > 0 else 1, abs(far) - 1)]
+                add((i, 4, j, 0, m), "pair", (0, 1), deps, unit * 2 * na * PAIR_LOAD, {a: None, b: off, c: far})
     return sends
 
 
@@ -124,11 +136,11 @@
         i, phase, j, s, d = k
         if phase == 4:
             return 0.0
-        extra = (0, 0, 2)[i]
+        extra = (0, 0, 6)[i]
         if phase == 3:
             b, c = streams[i][3][1:]
-            return 20 + extra - 2 * (SIZE[c] // 2 - d) + 0.3 * min(j, SIZE[b] - j)
-        return extra - d
+            return 5 + extra + (SIZE[c] // 2 - d) + 0.3 * min(j, SIZE[b] - j)
+        return extra + d
 
     order, arrive = timeline(sends, rank)
     return streams, sends, order, arrive
@@ -249,16 +261,18 @@
                 keep.wait()
                 kept = True
             copy(side, key).start()
-            if key[1] == 3 and "swap" not in done:
-                done.add("swap")
+            number = order.index(key)
+            if number == len(order) // 4:
                 swap.start()
+            if number == len(order) // 2:
                 keys_ref[...] = sort_keys(items_ref[...], blocks_ref[...])
                 used_ref[0:1, :] = used_panels(items_ref[...], used_ref.shape[1])
+            if number == 3 * len(order) // 4:
+                swap.wait()
+                used_ref[1:2, :] = used_panels(other_items[...], used_ref.shape[1])
         for key in sorted(order, key=lambda k: arrive[k]):
             if key[1] != 4 and key not in done:
                 copy(side, key).wait_recv()
-        swap.wait()
-        used_ref[1:2, :] = used_panels(other_items[...], used_ref.shape[1])
         for key in plans[1 - side][2]:
             if key[1] == 4:
                 copy(1 - side, key).wait_recv()
@@ -634,13 +648,16 @@
     def group(g, _):
         base = g * GROUP
         for n in range(GROUP):
-            i = base + n
-            for c in fetch(i):
+            for c in fetch(base + n):
                 c.wait()
 
-            @pl.when((i >= RING) & is_last(i - RING))
-            def _():
-                put(i - RING).wait()
+        @pl.when(base >= RING)
+        def _():
+            for n in range(GROUP):
+
+                @pl.when(is_last(base + n - RING))
+                def _():
+                    put(base + n - RING).wait()
 
         errs = []
         for n in range(GROUP):
@@ -670,9 +687,10 @@
             def _():
                 put(i).start()
 
-            @pl.when(i + RING < tiles)
-            def _():
-                for c in fetch(i + RING):
+        @pl.when(base + RING < tiles)
+        def _():
+            for n in range(GROUP):
+                for c in fetch(base + n + RING):
                     c.start()
 
         return 0

time: 137 us -> 140 us (1.022)
  Pallas kernels: 135 us -> 139 us
    pallas_call x1, Pallas kernels: 61 us -> 64.5 us  [gather_panels(): pl.pallas_call(functools.partial(gather_kernel, plans), out_shape=(jax.Sh...]
where the time goes in v4:
time: 140 us; the launch traced here: 139 us
  Pallas kernels  139 us (99%)
    pallas_call x1, Pallas kernels, gather_panels(): pl.pallas_call(functools.partial(gather_kernel, plans), out_shape=(jax.Sh...  64.5 us
    pallas_call x1, Pallas kernels, reduce_parts(): pl.pallas_call(reduce_kernel, out_shape=(jax.ShapeDtypeStruct(user_part.s...  53 us
    pallas_call x1, Pallas kernels, tile_parts(): pl.pallas_call(tiles_kernel, out_shape=(jax.ShapeDtypeStruct((128, 128, 2...  16.8 us
    pallas_call x1, Pallas kernels, adagrad(): pl.pallas_call(adagrad_kernel, grid=(steps,), out_shape=tuple((jax.ShapeD...  4.29 us

profile of v4, /device:TPU:1, one launch (start us, length us, event | category | flops | bytes accessed | tf_op | source)
XLA Modules:
  0.0 139.4 jit_solution(18094686489125685303)
XLA Ops:
  0.6 64.5 %gather_panels.1 = (bf16[8,4,4,2,128,256]{5,4,3,2,1,0:T(8,128)(2,1)}, s32[1,128]{1,0:T(1,128)}, s32[2,256]{1,0:T(2,128)}) custom-call(f32[256,256]{1,0:T(8,128)} %items.1, s32[1,128]{1,0:T(1,128)} %bitcast.17, s32[1,128]{1,0:T(1,128)} %bitcast.18), custom_call_target="tpu_custom_call" | custom-call | tf_op jit(solution)/shard_map/gather_panels/pallas_call | solution.py:291
  65.2 16.8 %tile_parts.1 = (bf16[128,128,256]{2,1,0:T(8,128)(2,1)}, f32[8,128,256]{2,1,0:T(8,128)}) custom-call(s32[128]{0:T(128)} %bitcast.16, bf16[256,128,256]{2,1,0:T(8,128)(2,1)} %bitcast.9, bf16[128,128,128]{2,1,0:T(8,128)(2,1)} %bitcast.14, f32[8,128,256]{2,1,0:T(8,128)} %bitcast.11), custom_call_target="tpu_custom_call" | custom-call | flops 3221225472 | bytes 27262976 | tf_op jit(solution)/shard_map/tile_parts/pallas_call | solution.py:715
  81.9 53.0 %reduce_parts.1 = (f32[1024,256]{1,0:T(8,128)}, f32[2,128,256]{2,1,0:T(8,128)}) custom-call(bf16[8,4,4,128,256]{4,3,2,1,0:T(8,128)(2,1)} %bitcast.10, s32[2,256]{1,0:T(2,128)} %get-tuple-element.15.used_ref, f32[1024,256]{1,0:T(8,128)} %bitcast.12), custom_call_target="tpu_custom_call" | custom-call | tf_op jit(solution)/shard_map/reduce_parts/pallas_call | solution.py:592
  134.9 4.3 %adagrad.1 = (f32[1024,256]{1,0:T(8,128)}, f32[1024,256]{1,0:T(8,128)}, f32[256,256]{1,0:T(8,128)}, f32[256,256]{1,0:T(8,128)}) custom-call(f32[1024,256]{1,0:T(8,128)} %bitcast.13, f32[1024,256]{1,0:T(8,128)} %get-tuple-element.16.other, f32[1024,256]{1,0:T(8,128)} %users.1, f32[1024,256]{1,0:T(8,128)} %user_accum.1, f32[256,256]{1,0:T(8,128)} %bitcast.15, ...), custom_call_target="tpu_custom_call" | custom-call | tf_op jit(solution)/shard_map/adagrad/pallas_call | solution.py:757

commit v5 on v4

--- a/solution.py
+++ b/solution.py
@@ -23,7 +23,6 @@
         (slice(1, 2), 0, 48, ("x", "z", "y")),
     ),
 )
-PAIR_LOAD = 5 / 3
 RATE, PAIR_RATE, HOP, PAIR_HOP, ISSUE, AHEAD = 43e3, 500e3, 1.7, 0.8, 0.07, 2.5
 
 
@@ -69,19 +68,8 @@
             for s, d, h in ring_steps(nc):
                 deps = line if d == 0 else [(i, 3, j, s, d - 1)]
                 add((i, 3, j, s, d), c, h, deps, unit * len(h) * na, {a: None, b: off, c: -s * d})
-            if abs(off) < nb // 2:
-                deps = line + [(i, 3, j, s, d) for s, d, h in ring_steps(nc)]
-                add((i, 4, j, 0, 0), "pair", (0, 1), deps, unit * 2 * na * nc * PAIR_LOAD, {a: None, b: off, c: None})
-                continue
-            for m in range(nc):
-                far = signed(m, nc)
-                if far == 0:
-                    deps = line
-                elif far == nc // 2:
-                    deps = [(i, 3, j, s, nc // 2 - 1) for s in (1, -1)]
-                else:
-                    deps = [(i, 3, j, -1 if far > 0 else 1, abs(far) - 1)]
-                add((i, 4, j, 0, m), "pair", (0, 1), deps, unit * 2 * na * PAIR_LOAD, {a: None, b: off, c: far})
+            deps = line + [(i, 3, j, s, d) for s, d, h in ring_steps(nc)]
+            add((i, 4, j, 0, 0), "pair", (0, 1), deps, unit * 2 * na * nc, {a: None, b: off, c: None})
     return sends
 
 
@@ -136,11 +124,10 @@
         i, phase, j, s, d = k
         if phase == 4:
             return 0.0
-        extra = (0, 0, 6)[i]
+        extra = (0, 6, 0)[i]
         if phase == 3:
-            b, c = streams[i][3][1:]
-            return 5 + extra + (SIZE[c] // 2 - d) + 0.3 * min(j, SIZE[b] - j)
-        return extra + d
+            return 20 + extra - 0.5 * (SIZE[streams[i][3][2]] // 2 - d)
+        return extra - d
 
     order, arrive = timeline(sends, rank)
     return streams, sends, order, arrive
@@ -748,7 +735,7 @@
         new[...] = factors[...] - g / jnp.sqrt(total)
 
 
-def adagrad(part, other, users, user_accum, grad, items, item_accum, steps=4):
+def adagrad(part, other, users, user_accum, grad, items, item_accum, steps=2):
     def rows(x):
         return pl.BlockSpec((x.shape[0] // steps, x.shape[1]), lambda n: (n, 0))
 

time: 140 us -> 137 us (0.979)
  Pallas kernels: 139 us -> 135 us
where the time goes in v5:
time: 137 us; the launch traced here: 136 us
  Pallas kernels  135 us (99%)
    pallas_call x1, Pallas kernels, gather_panels(): pl.pallas_call(functools.partial(gather_kernel, plans), out_shape=(jax.Sh...  63.2 us
    pallas_call x1, Pallas kernels, reduce_parts(): pl.pallas_call(reduce_kernel, out_shape=(jax.ShapeDtypeStruct(user_part.s...  51.7 us
    pallas_call x1, Pallas kernels, tile_parts(): pl.pallas_call(tiles_kernel, out_shape=(jax.ShapeDtypeStruct((128, 128, 2...  17 us
    pallas_call x1, Pallas kernels, adagrad(): pl.pallas_call(adagrad_kernel, grid=(steps,), out_shape=tuple((jax.ShapeD...  3.53 us

profile of v5, /device:TPU:1, one launch (start us, length us, event | category | flops | bytes accessed | tf_op | source)
XLA Modules:
  0.0 136.2 jit_solution(9660015874125493364)
XLA Ops:
  0.6 63.2 %gather_panels.1 = (bf16[8,4,4,2,128,256]{5,4,3,2,1,0:T(8,128)(2,1)}, s32[1,128]{1,0:T(1,128)}, s32[2,256]{1,0:T(2,128)}) custom-call(f32[256,256]{1,0:T(8,128)} %items.1, s32[1,128]{1,0:T(1,128)} %bitcast.17, s32[1,128]{1,0:T(1,128)} %bitcast.18), custom_call_target="tpu_custom_call" | custom-call | tf_op jit(solution)/shard_map/gather_panels/pallas_call | solution.py:278
  63.9 17.0 %tile_parts.1 = (bf16[128,128,256]{2,1,0:T(8,128)(2,1)}, f32[8,128,256]{2,1,0:T(8,128)}) custom-call(s32[128]{0:T(128)} %bitcast.16, bf16[256,128,256]{2,1,0:T(8,128)(2,1)} %bitcast.9, bf16[128,128,128]{2,1,0:T(8,128)(2,1)} %bitcast.14, f32[8,128,256]{2,1,0:T(8,128)} %bitcast.11), custom_call_target="tpu_custom_call" | custom-call | flops 3221225472 | bytes 27262976 | tf_op jit(solution)/shard_map/tile_parts/pallas_call | solution.py:702
  80.8 51.7 %reduce_parts.1 = (f32[1024,256]{1,0:T(8,128)}, f32[2,128,256]{2,1,0:T(8,128)}) custom-call(bf16[8,4,4,128,256]{4,3,2,1,0:T(8,128)(2,1)} %bitcast.10, s32[2,256]{1,0:T(2,128)} %get-tuple-element.15.used_ref, f32[1024,256]{1,0:T(8,128)} %bitcast.12), custom_call_target="tpu_custom_call" | custom-call | tf_op jit(solution)/shard_map/reduce_parts/pallas_call | solution.py:579
  132.6 3.5 %adagrad.1 = (f32[1024,256]{1,0:T(8,128)}, f32[1024,256]{1,0:T(8,128)}, f32[256,256]{1,0:T(8,128)}, f32[256,256]{1,0:T(8,128)}) custom-call(f32[1024,256]{1,0:T(8,128)} %bitcast.13, f32[1024,256]{1,0:T(8,128)} %get-tuple-element.16.other, f32[1024,256]{1,0:T(8,128)} %users.1, f32[1024,256]{1,0:T(8,128)} %user_accum.1, f32[256,256]{1,0:T(8,128)} %bitcast.15, ...), custom_call_target="tpu_custom_call" | custom-call | tf_op jit(solution)/shard_map/adagrad/pallas_call | solution.py:744
